TPU v7x, 32 devices: a whole 2x2x4 slice. The times are simulated.
32 devices in a mesh: seq: 16 (over z, x, core), tok: 2 (over y).
Axes of the slice: x: 2, y: 2, z: 4, core: 2. Of those that a mesh axis runs over, the one named last changes fastest.
Arguments:
- tokens: bfloat16 [128, 128, 1024], P('seq', 'tok'), may hold values from -6 to 6
- noise_times: int32 [128], P('seq'), may hold values from 0 to 999
- time_proj: bfloat16 [256, 1024], replicated, may hold values from -0.375 to 0.375
- time_bias: bfloat16 [1024], replicated, may hold values from -1.5 to 1.5
- gain_one: bfloat16 [1024], replicated, may hold values from 0.5 to 1.5
- shift_one: bfloat16 [1024], replicated, may hold values from -1.5 to 1.5
- w_qkv: bfloat16 [1024, 3072], replicated, may hold values from -0.1875 to 0.1875
- w_out: bfloat16 [1024, 1024], replicated, may hold values from -1.25 to 1.25
- gain_two: bfloat16 [1024], replicated, may hold values from 0.5 to 1.5
- shift_two: bfloat16 [1024], replicated, may hold values from -1.5 to 1.5
- w_up: bfloat16 [1024, 4096], replicated, may hold values from -0.1875 to 0.1875
- b_up: bfloat16 [4096], replicated, may hold values from -2.5 to 2.5
- w_down: bfloat16 [4096, 1024], replicated, may hold values from -0.09375 to 0.09375
- b_down: bfloat16 [1024], replicated, may hold values from -1.5 to 1.5
- cotangent: bfloat16 [128, 128, 1024], P('seq', 'tok'), may hold values from -6 to 6
Outputs:
- mixed_out: bfloat16 [128, 128, 1024], P('seq', 'tok')
- grad_tokens: bfloat16 [128, 128, 1024], P('seq', 'tok')
- grad_time_proj: float32 [256, 1024], P(None, 'seq')
- grad_time_bias: float32 [1024], P('seq')
- grad_gain_one: float32 [1024], P('seq')
- grad_shift_one: float32 [1024], P('seq')
- grad_w_qkv: float32 [1024, 3072], P(None, 'seq')
- grad_w_out: float32 [1024, 1024], P(None, 'seq')
- grad_gain_two: float32 [1024], P('seq')
- grad_shift_two: float32 [1024], P('seq')
- grad_w_up: float32 [1024, 4096], P(None, 'seq')
- grad_b_up: float32 [4096], P('seq')
- grad_w_down: float32 [4096, 1024], P(None, 'seq')
- grad_b_down: float32 [1024], P('seq')
All inputs are finite; a program needn't handle non-finite values.
Results may differ from a plain program's by a relative error of at most 0.017.
Values may be sent and summed in bfloat16 or wider, within the bound.
A program may use at most 256 MiB of HBM per device.

v0:
```python
import math

import jax
import jax.numpy as jnp
from jax import lax
from jax.sharding import PartitionSpec as P

HD = 64
TEMB = 256


def layer_norm(hidden, gain_vec, shift_vec):
    center = hidden - jnp.mean(hidden, axis=-1, keepdims=True)
    spread = jnp.mean(center * center, axis=-1, keepdims=True)
    return center * lax.rsqrt(spread + 1e-05) * gain_vec + shift_vec


def noise_table(noise_steps):
    halves = TEMB // 2
    frequency = jnp.exp(-math.log(10000.0) * jnp.arange(halves, dtype=jnp.float32) / halves)
    angles = noise_steps.astype(jnp.float32)[:, None] * frequency[None, :]
    return jnp.concatenate([jnp.sin(angles), jnp.cos(angles)], axis=-1)


def rotary_tables(length):
    halves = HD // 2
    frequency = jnp.exp(-math.log(10000.0) * jnp.arange(halves, dtype=jnp.float32) / halves)
    angles = jnp.arange(length, dtype=jnp.float32)[:, None] * frequency[None, :]
    angles = jnp.concatenate([angles, angles], axis=-1)[:, None, :]
    return (jnp.cos(angles), jnp.sin(angles))


def rotate(values, cosine, sine_tab):
    halves = values.shape[-1] // 2
    turned = jnp.concatenate([-values[..., halves:], values[..., :halves]], axis=-1)
    return values * cosine + turned * sine_tab


def unrotate(gradient, cosine, sine_tab):
    halves = gradient.shape[-1] // 2
    scaled = gradient * sine_tab
    turned = jnp.concatenate([scaled[..., halves:], -scaled[..., :halves]], axis=-1)
    return gradient * cosine + turned


def product(left_side, right_side):
    return jnp.dot(left_side, right_side, preferred_element_type=jnp.float32)


def contract_rows(left_side, right_side):
    return jnp.einsum("ra,rb->ab", left_side, right_side, preferred_element_type=jnp.float32)


def times_transpose(left_side, right_side):
    return jnp.einsum("rb,ab->ra", left_side, right_side, preferred_element_type=jnp.float32)


def split_heads(received):
    batch_size, length = (received.shape[0], received.shape[1])
    local_heads = received.shape[-1] // HD
    split_view = received.reshape(batch_size, length, 3, local_heads, HD)
    cosine, sine_tab = rotary_tables(length)
    queries = rotate(split_view[:, :, 0].astype(jnp.float32), cosine, sine_tab).astype(jnp.bfloat16)
    keys_rot = rotate(split_view[:, :, 1].astype(jnp.float32), cosine, sine_tab).astype(
        jnp.bfloat16
    )
    return (queries, keys_rot, split_view[:, :, 2], cosine, sine_tab)


def attend_items(received):
    batch_size, length = (received.shape[0], received.shape[1])
    scaling = 1.0 / math.sqrt(HD)
    queries, keys_rot, values, cosine, sine_tab = split_heads(received)
    scores = (
        jnp.einsum("gqhd,gkhd->ghqk", queries, keys_rot, preferred_element_type=jnp.float32)
        * scaling
    )
    highest = jnp.max(scores, axis=-1, keepdims=True)
    exponent = jnp.exp(scores - highest)
    totals = jnp.sum(exponent, axis=-1, keepdims=True)
    prob_rows = (exponent / totals).astype(jnp.bfloat16)
    log_total = (highest + jnp.log(totals))[..., 0]
    attended = jnp.einsum("ghqk,gkhd->gqhd", prob_rows, values, preferred_element_type=jnp.float32)
    attended = attended.astype(jnp.bfloat16).reshape(batch_size, length, 1, -1)
    return (received, attended, log_total)


def attention_grad(received, log_total, grad_heads):
    batch_size, length = (received.shape[0], received.shape[1])
    scaling = 1.0 / math.sqrt(HD)
    queries, keys_rot, values, cosine, sine_tab = split_heads(received)
    scores = (
        jnp.einsum("gqhd,gkhd->ghqk", queries, keys_rot, preferred_element_type=jnp.float32)
        * scaling
    )
    prob_rows = jnp.exp(scores - log_total[..., None])
    grad_out = grad_heads.reshape(batch_size, length, values.shape[2], HD)
    grad_probs = jnp.einsum("gqhd,gkhd->ghqk", grad_out, values, preferred_element_type=jnp.float32)
    grad_values = jnp.einsum(
        "ghqk,gqhd->gkhd",
        prob_rows.astype(jnp.bfloat16),
        grad_out,
        preferred_element_type=jnp.float32,
    )
    inner_sum = jnp.sum(prob_rows * grad_probs, axis=-1, keepdims=True)
    grad_scores = (prob_rows * (grad_probs - inner_sum)).astype(jnp.bfloat16)
    grad_queries = (
        jnp.einsum("ghqk,gkhd->gqhd", grad_scores, keys_rot, preferred_element_type=jnp.float32)
        * scaling
    )
    grad_keys = (
        jnp.einsum("ghqk,gqhd->gkhd", grad_scores, queries, preferred_element_type=jnp.float32)
        * scaling
    )
    stacked = jnp.stack(
        [
            unrotate(grad_queries, cosine, sine_tab),
            unrotate(grad_keys, cosine, sine_tab),
            grad_values,
        ],
        axis=2,
    )
    return stacked.astype(jnp.bfloat16).reshape(batch_size, length, 3, 1, -1)


def body(
    tokens,
    noise_times,
    time_proj,
    time_bias,
    gain_one,
    shift_one,
    w_qkv,
    w_out,
    gain_two,
    shift_two,
    w_up,
    b_up,
    w_down,
    b_down,
    cotangent,
):
    seq_count, sub_len, model_width = tokens.shape
    tok_ways = lax.axis_size("tok")
    row_count = seq_count * sub_len
    embed_table = noise_table(noise_times).astype(jnp.bfloat16)
    time_embed = product(embed_table, time_proj) + time_bias.astype(jnp.float32)
    hidden_zero = (tokens.astype(jnp.float32) + time_embed[:, None, :]).reshape(
        row_count, model_width
    )
    normed_one, pull_one = jax.vjp(
        layer_norm, hidden_zero, gain_one.astype(jnp.float32), shift_one.astype(jnp.float32)
    )
    normed_one = normed_one.astype(jnp.bfloat16)
    projected = (
        product(normed_one, w_qkv).astype(jnp.bfloat16).reshape(seq_count, sub_len, 3, tok_ways, -1)
    )
    received, attended, log_total = attend_items(
        lax.all_to_all(projected, "tok", split_axis=3, concat_axis=1, tiled=True)
    )
    attended = lax.all_to_all(attended, "tok", split_axis=1, concat_axis=2, tiled=True).reshape(
        row_count, model_width
    )
    hidden_one = hidden_zero + product(attended, w_out)
    normed_two, pull_two = jax.vjp(
        layer_norm, hidden_one, gain_two.astype(jnp.float32), shift_two.astype(jnp.float32)
    )
    normed_two = normed_two.astype(jnp.bfloat16)
    upward = product(normed_two, w_up) + b_up.astype(jnp.float32)
    active, pull_gelu = jax.vjp(jax.nn.gelu, upward)
    active = active.astype(jnp.bfloat16)
    result = hidden_one + (product(active, w_down) + b_down.astype(jnp.float32))
    incoming = cotangent.reshape(row_count, model_width)
    sum_down = jnp.sum(incoming, axis=0, dtype=jnp.float32)
    grad_w_down = contract_rows(active, incoming)
    grad_active = times_transpose(incoming, w_down)
    (grad_upward,) = pull_gelu(grad_active)
    grad_upward = grad_upward.astype(jnp.bfloat16)
    sum_up = jnp.sum(grad_upward, axis=0, dtype=jnp.float32)
    grad_w_up = contract_rows(normed_two, grad_upward)
    grad_norm_two = times_transpose(grad_upward, w_up)
    grad_hidden_two, grad_gain_two, grad_shift_two = pull_two(grad_norm_two)
    grad_hidden_one = incoming.astype(jnp.float32) + grad_hidden_two
    grad_attn = grad_hidden_one.astype(jnp.bfloat16)
    grad_w_out = contract_rows(attended, grad_attn)
    grad_mixed = (
        times_transpose(grad_attn, w_out)
        .astype(jnp.bfloat16)
        .reshape(seq_count, sub_len, tok_ways, -1)
    )
    grad_heads = lax.all_to_all(grad_mixed, "tok", split_axis=2, concat_axis=1, tiled=True)
    grad_parts = attention_grad(received, log_total, grad_heads)
    grad_parts = lax.all_to_all(grad_parts, "tok", split_axis=1, concat_axis=3, tiled=True).reshape(
        row_count, 3 * model_width
    )
    grad_w_qkv = contract_rows(normed_one, grad_parts)
    grad_norm_one = times_transpose(grad_parts, w_qkv)
    grad_hidden_zero, grad_gain_one, grad_shift_one = pull_one(grad_norm_one)
    grad_total = grad_hidden_one + grad_hidden_zero
    grad_tokens = grad_total.astype(jnp.bfloat16).reshape(seq_count, sub_len, model_width)
    grad_embed = jnp.sum(grad_total.reshape(seq_count, sub_len, model_width), axis=1)
    grad_time_bias = jnp.sum(grad_embed, axis=0)
    grad_time_proj = jnp.dot(
        embed_table.astype(jnp.float32).T, grad_embed, precision=lax.Precision.HIGHEST
    )
    summed = (
        lax.psum_scatter(
            grad_time_proj.astype(jnp.bfloat16), "seq", scatter_dimension=1, tiled=True
        ).astype(jnp.float32),
        lax.psum_scatter(
            grad_time_bias[None, :].astype(jnp.bfloat16), "seq", scatter_dimension=1, tiled=True
        ).astype(jnp.float32),
        lax.psum_scatter(
            grad_gain_one[None, :].astype(jnp.bfloat16), "seq", scatter_dimension=1, tiled=True
        ).astype(jnp.float32),
        lax.psum_scatter(
            grad_shift_one[None, :].astype(jnp.bfloat16), "seq", scatter_dimension=1, tiled=True
        ).astype(jnp.float32),
        lax.psum_scatter(
            grad_w_qkv.astype(jnp.bfloat16), "seq", scatter_dimension=1, tiled=True
        ).astype(jnp.float32),
        lax.psum_scatter(
            grad_w_out.astype(jnp.bfloat16), "seq", scatter_dimension=1, tiled=True
        ).astype(jnp.float32),
        lax.psum_scatter(
            grad_gain_two[None, :].astype(jnp.bfloat16), "seq", scatter_dimension=1, tiled=True
        ).astype(jnp.float32),
        lax.psum_scatter(
            grad_shift_two[None, :].astype(jnp.bfloat16), "seq", scatter_dimension=1, tiled=True
        ).astype(jnp.float32),
        lax.psum_scatter(
            grad_w_up.astype(jnp.bfloat16), "seq", scatter_dimension=1, tiled=True
        ).astype(jnp.float32),
        lax.psum_scatter(
            sum_up[None, :].astype(jnp.bfloat16), "seq", scatter_dimension=1, tiled=True
        ).astype(jnp.float32),
        lax.psum_scatter(
            grad_w_down.astype(jnp.bfloat16), "seq", scatter_dimension=1, tiled=True
        ).astype(jnp.float32),
        lax.psum_scatter(
            sum_down[None, :].astype(jnp.bfloat16), "seq", scatter_dimension=1, tiled=True
        ).astype(jnp.float32),
    )
    summed = (
        lax.psum(summed[0].astype(jnp.bfloat16), "tok").astype(jnp.float32),
        lax.psum(summed[1].astype(jnp.bfloat16), "tok").astype(jnp.float32),
        lax.psum(summed[2].astype(jnp.bfloat16), "tok").astype(jnp.float32),
        lax.psum(summed[3].astype(jnp.bfloat16), "tok").astype(jnp.float32),
        lax.psum(summed[4].astype(jnp.bfloat16), "tok").astype(jnp.float32),
        lax.psum(summed[5].astype(jnp.bfloat16), "tok").astype(jnp.float32),
        lax.psum(summed[6].astype(jnp.bfloat16), "tok").astype(jnp.float32),
        lax.psum(summed[7].astype(jnp.bfloat16), "tok").astype(jnp.float32),
        lax.psum(summed[8].astype(jnp.bfloat16), "tok").astype(jnp.float32),
        lax.psum(summed[9].astype(jnp.bfloat16), "tok").astype(jnp.float32),
        lax.psum(summed[10].astype(jnp.bfloat16), "tok").astype(jnp.float32),
        lax.psum(summed[11].astype(jnp.bfloat16), "tok").astype(jnp.float32),
    )
    out_proj, out_wqkv, out_wout, out_wup, out_wdown = (
        summed[0],
        summed[4],
        summed[5],
        summed[8],
        summed[10],
    )
    out_vectors = (
        summed[1][0],
        summed[2][0],
        summed[3][0],
        summed[6][0],
        summed[7][0],
        summed[9][0],
        summed[11][0],
    )
    mixed_out = result.astype(jnp.bfloat16).reshape(seq_count, sub_len, model_width)
    return (
        mixed_out,
        grad_tokens,
        out_proj,
        out_vectors[0],
        out_vectors[1],
        out_vectors[2],
        out_wqkv,
        out_wout,
        out_vectors[3],
        out_vectors[4],
        out_wup,
        out_vectors[5],
        out_wdown,
        out_vectors[6],
    )


def solution(mesh):
    in_specs = (
        P("seq", "tok", None),
        P("seq"),
        P(),
        P(),
        P(),
        P(),
        P(),
        P(),
        P(),
        P(),
        P(),
        P(),
        P(),
        P(),
        P("seq", "tok", None),
    )
    out_specs = (
        P("seq", "tok", None),
        P("seq", "tok", None),
        P(None, "seq"),
        P("seq"),
        P("seq"),
        P("seq"),
        P(None, "seq"),
        P(None, "seq"),
        P("seq"),
        P("seq"),
        P(None, "seq"),
        P("seq"),
        P(None, "seq"),
        P("seq"),
    )
    return jax.shard_map(body, mesh=mesh, in_specs=in_specs, out_specs=out_specs, check_vma=False)
```

profile of v0, /device:TPU:0, one launch (start us, length us, event | category | flops | bytes accessed | tf_op | source)
XLA Modules:
  0.0 1085.2 jit_solution(11585868900458624208)
XLA Ops:
  24.3 8.3 reshape.363
  36.9 5.4 all-to-all-start
  42.7 37.3 %all-to-all-done = bf16[8,64,3,2,512]{4,1,2,0,3:T(8,128)(2,1)} async-done(((bf16[8,64,3,2,512]{4,1,2,0,3:T(8,128)(2,1)}), bf16[8,64,3,2,512]{4,1,2,0,3:T(8,128)(2,1)}, u32[]{:S(2)}, u32[]{:S(2)}) %all-to-all-start) | async-done | bytes 3145760 | tf_op jit(solution)/shard_map/all_to_all | solution.py:159
  83.9 8.9 reshape.364
  92.8 7.1 fusion.47
  102.9 8.8 slice_negate_fusion
  111.7 5.8 fusion.10
  138.7 10.9 %all-to-all-done.1 = bf16[8,128,1,512]{3,0,2,1:T(8,128)(2,1)} async-done(((bf16[8,128,1,512]{3,0,2,1:T(8,128)(2,1)}), bf16[8,128,1,512]{3,0,2,1:T(8,128)(2,1)}, u32[]{:S(2)}, u32[]{:S(2)}) %all-to-all-start.1) | async-done | bytes 1048608 | tf_op jit(solution)/shard_map/all_to_all | solution.py:161
  157.1 7.5 fusion.41
  164.6 15.4 %fusion.42 = (bf16[4096]{0:T(1024)(128)(2,1)S(1)}, bf16[512,4096]{1,0:T(8,128)(2,1)}) fusion(f32[512,4096]{1,0:T(8,128)} %fusion.41, f32[4096]{0:T(1024)S(1)} %convert_element_type.286, bf16[512,1024]{1,0:T(8,128)(2,1)S(1)} %bitcast.145, bf16[4096,1024]{1,0:T(8,128)(2,1)} %param.27), kind=kOutput, calls=%fused_computation.115 | convolution fusion | flops 4341100544 | bytes 22044672 | tf_op jit(solution)/shard_map/rb,ab->ra/dot_general | solution.py:55
  180.0 7.5 multiply_reduce_fusion.2
  204.1 8.4 all-to-all-done.2
  220.1 5.0 fusion.23
  245.5 37.1 %all_to_all.60 = bf16[8,128,3,1,512]{4,0,3,2,1:T(8,128)(2,1)S(1)} all-to-all(bf16[8,128,3,1,512]{4,0,3,2,1:T(8,128)(2,1)S(1)} %pad_maximum_fusion), channel_id=1, replica_groups=mesh['seq'=16,'tok'=2] {'tok'}, dimensions={1} | all-to-all | bytes 6291456 | tf_op jit(solution)/shard_map/all_to_all | solution.py:193
  288.6 8.3 reshape.371
  296.9 7.3 convolution_convert_fusion.2
  305.4 11.7 %convolution_convert_fusion = bf16[4096,1024]{0,1:T(8,128)(2,1)} fusion(bf16[512,1024]{1,0:T(8,128)(2,1)S(1)} %bitcast.146, f32[512,4096]{1,0:T(8,128)} %fusion.41, f32[4096]{0:T(1024)S(1)} %convert_element_type.286), kind=kOutput, calls=%fused_computation.10 | convolution fusion | flops 4320133120 | bytes 17842176 | tf_op jit(solution)/shard_map/ra,rb->ab/dot_general | solution.py:51
  318.9 9.5 convolution_convert_fusion.1
  332.2 7.7 multiply_reduce_fusion.3
  348.0 41.2 %reduce-scatter.29.cloned.1.call-done = bf16[1024,192]{0,1:T(8,128)(2,1)} async-done(((bf16[1024,3072]{0,1:T(8,128)(2,1)}), bf16[1024,192]{0,1:T(8,128)(2,1)}) %reduce-scatter.29.cloned.1.call-update) | async-done | bytes 393232 | tf_op jit(solution)/shard_map/reduce_scatter | solution.py:219
  389.1 107.7 %reduce-scatter.35.cloned.1.call-done = bf16[4096,64]{0,1:T(8,128)(2,1)} async-done(((bf16[4096,1024]{0,1:T(8,128)(2,1)}), bf16[4096,64]{0,1:T(8,128)(2,1)}) %reduce-scatter.35.cloned.1.call-update) | async-done | bytes 524304 | tf_op jit(solution)/shard_map/reduce_scatter | solution.py:237
  496.8 108.5 %reduce-scatter.33.cloned.1.call-done = bf16[1024,256]{1,0:T(8,128)(2,1)} async-done(((bf16[1024,4096]{1,0:T(8,128)(2,1)}), bf16[1024,256]{1,0:T(8,128)(2,1)}) %reduce-scatter.33.cloned.1.call-update) | async-done | bytes 524304 | tf_op jit(solution)/shard_map/reduce_scatter | solution.py:231
  605.4 12.8 %add_convert_fusion.1 = bf16[512,1024]{1,0:T(8,128)(2,1)} fusion(f32[512,1024]{1,0:T(8,128)} %copy-done.14, bf16[4096,1024]{1,0:T(8,128)(2,1)} %param.27, f32[1024]{0:T(1024)S(1)} %convert_element_type.288, f32[512,4096]{1,0:T(8,128)} %fusion.41, f32[4096]{0:T(1024)S(1)} %convert_element_type.286), kind=kOutput, calls=%fused_computation.57 | convolution fusion | flops 4317511680 | bytes 19943424 | tf_op jit(solution)/shard_map/dot_general | solution.py:47
  618.2 46.2 %reduce-scatter.43.cloned.1.call-done = bf16[64,1]{1,0:T(8,128)(2,1)} async-done(((bf16[1024,1]{1,0:T(8,128)(2,1)}), bf16[64,1]{1,0:T(8,128)(2,1)}) %reduce-scatter.43.cloned.1.call-update) | async-done | bytes 144
  665.2 57.1 %reduce-scatter.45.cloned.1.call-done = bf16[64,1]{1,0:T(8,128)(2,1)} async-done(((bf16[1024,1]{1,0:T(8,128)(2,1)}), bf16[64,1]{1,0:T(8,128)(2,1)}) %reduce-scatter.45.cloned.1.call-update) | async-done | bytes 144
  723.0 59.9 %reduce-scatter.47.cloned.1.call-done = bf16[256,1]{1,0:T(8,128)(2,1)} async-done(((bf16[4096,1]{1,0:T(8,128)(2,1)}), bf16[256,1]{1,0:T(8,128)(2,1)}) %reduce-scatter.47.cloned.1.call-update) | async-done | bytes 528
  786.7 55.0 %reduce-scatter.37.cloned.1.call-done = bf16[64,1]{1,0:T(8,128)(2,1)} async-done(((bf16[1024,1]{1,0:T(8,128)(2,1)}), bf16[64,1]{1,0:T(8,128)(2,1)}) %reduce-scatter.37.cloned.1.call-update) | async-done | bytes 144
  842.5 58.0 %reduce-scatter.39.cloned.1.call-done = bf16[64,1]{1,0:T(8,128)(2,1)} async-done(((bf16[1024,1]{1,0:T(8,128)(2,1)}), bf16[64,1]{1,0:T(8,128)(2,1)}) %reduce-scatter.39.cloned.1.call-update) | async-done | bytes 144
  901.3 57.5 %reduce-scatter.41.cloned.1.call-done = bf16[64,1]{1,0:T(8,128)(2,1)} async-done(((bf16[1024,1]{1,0:T(8,128)(2,1)}), bf16[64,1]{1,0:T(8,128)(2,1)}) %reduce-scatter.41.cloned.1.call-update) | async-done | bytes 144
  959.6 58.4 %reduce-scatter.27.cloned.1.call-done = bf16[256,64]{0,1:T(8,128)(2,1)} async-done(((bf16[256,1024]{0,1:T(8,128)(2,1)}), bf16[256,64]{0,1:T(8,128)(2,1)}) %reduce-scatter.27.cloned.1.call-update) | async-done | bytes 32784 | tf_op jit(solution)/shard_map/reduce_scatter | solution.py:207
  1018.1 9.2 all-reduce
  1031.6 40.1 %all-reduce.4.cloned.1.call-done = (bf16[1024,192]{0,1:T(8,128)(2,1)}, bf16[1024,64]{0,1:T(8,128)(2,1)}, bf16[1024,256]{1,0:T(8,128)(2,1)}, bf16[4096,64]{0,1:T(8,128)(2,1)}) async-done(((bf16[1024,192]{0,1:T(8,128)(2,1)}, bf16[1024,64]{0,1:T(8,128)(2,1)}, bf16[1024,256]{1,0:T(8,128)(2,1)}, bf16[4096,64]{0,1:T(8,128)(2,1)}), (bf16[1024,192]{0,1:T(8,128)(2,1)}, bf16[1024,64]{0,1:T(8,128)(2,1)}, ...) | async-done | bytes 1572880 | tf_op jit(solution)/shard_map/psum | solution.py:249
  (225 shorter events, 141.0 us)
Async XLA Ops:
  7.2 145.5 %copy-start = (bf16[1024,1024]{1,0:T(8,128)(2,1)S(1)}, bf16[1024,1024]{1,0:T(8,128)(2,1)}, u32[]{:S(2)}) copy-start(bf16[1024,1024]{1,0:T(8,128)(2,1)} %param.22) | copy-start | bytes 6291460
  7.2 8.2 copy-start.10
  12.3 6.4 copy-start.30
  36.9 43.0 %all-to-all-start = ((bf16[8,64,3,2,512]{4,1,2,0,3:T(8,128)(2,1)}), bf16[8,64,3,2,512]{4,1,2,0,3:T(8,128)(2,1)}, u32[]{:S(2)}, u32[]{:S(2)}) async-start(bf16[8,64,3,2,512]{4,1,2,0,3:T(8,128)(2,1)} %copy.83), calls=%async_computation | async-start | bytes 6291456 | tf_op jit(solution)/shard_map/all_to_all | solution.py:159
  129.1 9.5 copy-start.41
  129.1 9.6 copy-start.42
  129.1 9.6 copy-start.40
  131.8 17.8 %all-to-all-start.1 = ((bf16[8,128,1,512]{3,0,2,1:T(8,128)(2,1)}), bf16[8,128,1,512]{3,0,2,1:T(8,128)(2,1)}, u32[]{:S(2)}, u32[]{:S(2)}) async-start(bf16[8,128,1,512]{3,0,2,1:T(8,128)(2,1)} %copy.92), calls=%async_computation.1 | async-start | bytes 2097152 | tf_op jit(solution)/shard_map/all_to_all | solution.py:161
  136.3 210.9 %reduce-scatter.49.cloned.1.call-start = ((), (), s32[]{:S(2)}) async-start(), calls=%async_computation.27 | async-start | bytes 278528
  154.1 33.4 %copy-start.14 = (f32[512,1024]{1,0:T(8,128)}, f32[512,1024]{1,0:T(8,128)S(1)}, u32[]{:S(2)}) copy-start(f32[512,1024]{1,0:T(8,128)S(1)} %get-tuple-element.70) | copy-start | bytes 6291460
  157.1 7.5 copy-start.12
  193.2 7.0 copy-start.24
  196.3 16.1 %all-to-all-start.2 = ((bf16[8,64,2,512]{3,1,0,2:T(8,128)(2,1)}), bf16[8,64,2,512]{3,1,0,2:T(8,128)(2,1)S(1)}, u32[]{:S(2)}, u32[]{:S(2)}) async-start(bf16[8,64,2,512]{3,1,0,2:T(8,128)(2,1)} %copy.95), calls=%async_computation.2 | async-start | bytes 2097152 | tf_op jit(solution)/shard_map/all_to_all | solution.py:191
  200.1 147.9 %reduce-scatter.31.cloned.1.call-start = ((), (), s32[]{:S(2)}) async-start(), calls=%async_computation.18 | async-start | bytes 2228224 | tf_op jit(solution)/shard_map/reduce_scatter | solution.py:222
  204.0 185.1 %reduce-scatter.29.cloned.1.call-start = ((), (), s32[]{:S(2)}) async-start(), calls=%async_computation.17 | async-start | bytes 6684672 | tf_op jit(solution)/shard_map/reduce_scatter | solution.py:219
  220.1 5.0 copy-start.3
  288.6 8.3 copy-start.25
  304.2 192.5 %reduce-scatter.35.cloned.1.call-start = ((), (), s32[]{:S(2)}) async-start(), calls=%async_computation.20 | async-start | bytes 8912896 | tf_op jit(solution)/shard_map/reduce_scatter | solution.py:237
  317.1 288.2 %reduce-scatter.33.cloned.1.call-start = ((), (), s32[]{:S(2)}) async-start(), calls=%async_computation.19 | async-start | bytes 8912896 | tf_op jit(solution)/shard_map/reduce_scatter | solution.py:231
  328.4 335.9 %reduce-scatter.43.cloned.1.call-start = ((), (), s32[]{:S(2)}) async-start(), calls=%async_computation.24 | async-start | bytes 278528
  329.4 392.8 %reduce-scatter.45.cloned.1.call-start = ((), (), s32[]{:S(2)}) async-start(), calls=%async_computation.25 | async-start | bytes 278528
  330.4 452.5 %reduce-scatter.47.cloned.1.call-start = ((), (), s32[]{:S(2)}) async-start(), calls=%async_computation.26 | async-start | bytes 1114112
  332.1 7.8 copy-start.39
  332.1 509.7 %reduce-scatter.37.cloned.1.call-start = ((), (), s32[]{:S(2)}) async-start(), calls=%async_computation.21 | async-start | bytes 278528
  342.0 263.4 %copy-start.9 = (f32[512,1024]{1,0:T(8,128)}, f32[512,1024]{1,0:T(8,128)S(1)}, u32[]{:S(2)}) copy-start(f32[512,1024]{1,0:T(8,128)S(1)} %get-tuple-element.35) | copy-start | bytes 6291460
  342.0 5.1 copy-start.43
  343.4 557.1 %reduce-scatter.39.cloned.1.call-start = ((), (), s32[]{:S(2)}) async-start(), calls=%async_computation.22 | async-start | bytes 278528
  344.6 614.3 %reduce-scatter.41.cloned.1.call-start = ((), (), s32[]{:S(2)}) async-start(), calls=%async_computation.23 | async-start | bytes 278528
  345.5 672.5 %reduce-scatter.27.cloned.1.call-start = ((), (), s32[]{:S(2)}) async-start(), calls=%async_computation.16 | async-start | bytes 557056 | tf_op jit(solution)/shard_map/reduce_scatter | solution.py:207
  347.1 724.6 %all-reduce.4.cloned.1.call-start = ((), (), s32[]{:S(2)}) async-start(), calls=%async_computation.28 | async-start | bytes 3145728 | tf_op jit(solution)/shard_map/psum | solution.py:249
  783.9 294.6 %copy-start.1 = (bf16[1024,1024]{1,0:T(8,128)(2,1)S(1)}, bf16[1024,1024]{1,0:T(8,128)(2,1)}, u32[]{:S(2)}) copy-start(bf16[1024,1024]{1,0:T(8,128)(2,1)} %param.22) | copy-start | bytes 6291460
  1071.7 5.7 copy-start.27
  (31 other events, 81.2 us)
Sparse Core Ops, SparseCore 0:
  140.6 57.2 reduce-scatter.48
  204.7 63.1 reduce-scatter.30
  304.4 84.7 reduce-scatter.28
  393.0 103.7 reduce-scatter.34
  500.7 104.5 reduce-scatter.32
  609.3 55.0 reduce-scatter.42
  667.9 54.3 reduce-scatter.44
  726.4 56.4 reduce-scatter.46
  787.4 54.2 reduce-scatter.36
  846.1 54.3 reduce-scatter.38
  904.4 54.3 reduce-scatter.40
  963.2 54.7 reduce-scatter.26
  1020.5 51.0 all-reduce.3
where the time goes:
time: 1090 us
  waiting for transfers between devices  746 us (68%)
  matrix products  109 us (10%)
  local copies, waits for them, and re-layouts  95.8 us (9%)
  other arithmetic  57.8 us (5%)
  blocking collectives  46.3 us (4%)
  between operations  14.8 us (1%)
  starting transfers between devices  14.7 us (1%)
    unnamed x20, waiting for transfers between devices  334 us
    reduce_scatter x1, waiting for transfers between devices, body(): lax.psum_scatter(grad_w_up.astype(jnp.bfloat16), 'seq', scatter_dimension...  109 us
    reduce_scatter x1, waiting for transfers between devices, body(): lax.psum_scatter(grad_w_down.astype(jnp.bfloat16), 'seq', scatter_dimensi...  108 us
    reduce_scatter x1, waiting for transfers between devices, body(): lax.psum_scatter(grad_time_proj.astype(jnp.bfloat16), 'seq', scatter_dime...  58.4 us
    reduce_scatter x1, waiting for transfers between devices, body(): lax.psum_scatter(grad_w_qkv.astype(jnp.bfloat16), 'seq', scatter_dimensio...  41.2 us
    psum x1, waiting for transfers between devices, body(): lax.psum(summed[4].astype(jnp.bfloat16), 'tok').astype(jnp.float32)  40.1 us
    all_to_all x1, waiting for transfers between devices, body(): lax.all_to_all(projected, 'tok', split_axis=3, concat_axis=1, tiled=True)  37.3 us
    all_to_all x1, blocking collectives, body(): lax.all_to_all(grad_parts, 'tok', split_axis=1, concat_axis=3, tiled=True)  37.1 us
  transfers between devices with their start and end apart: 16, of which 14 were waited for; matrix products, arithmetic and copies ran while one was open for 15% of the time, Pallas kernels for 0%

commit v1 on v0

--- a/solution.py
+++ b/solution.py
@@ -121,6 +121,68 @@
         axis=2,
     )
     return stacked.astype(jnp.bfloat16).reshape(batch_size, length, 3, 1, -1)
+
+
+def gather_sequences(values):
+    return lax.all_to_all(values, "tok", split_axis=0, concat_axis=1, tiled=True)
+
+
+def return_positions(values):
+    return lax.all_to_all(values, "tok", split_axis=1, concat_axis=0, tiled=True)
+
+
+def group_scatter(parts, own, size, axis, perm_of):
+    total = lax.dynamic_index_in_dim(parts, own, 0, keepdims=False).astype(jnp.float32)
+    for shift in range(1, size):
+        piece = lax.dynamic_index_in_dim(parts, (own + shift) % size, 0, keepdims=False)
+        total = total + lax.ppermute(piece, axis, perm_of(shift)).astype(jnp.float32)
+    return total.astype(jnp.bfloat16)
+
+
+def group_gather(piece, own, size, axis, perm_of):
+    held = jnp.zeros((size,) + piece.shape, piece.dtype)
+    held = lax.dynamic_update_index_in_dim(held, piece, own, 0)
+    for shift in range(1, size):
+        other = lax.ppermute(piece, axis, perm_of(shift))
+        held = lax.dynamic_update_index_in_dim(held, other, (own - shift) % size, 0)
+    return held
+
+
+def scatter_sum(gradient):
+    seq_ways, tok_ways = lax.axis_size("seq"), lax.axis_size("tok")
+    outer, middle = 4, seq_ways // 8
+    place, turn = lax.axis_index("seq"), lax.axis_index("tok")
+    core, mid, out = place % 2, (place // 2) % middle, place // (2 * middle)
+
+    def core_perm(shift):
+        return [(i, i ^ 1) for i in range(seq_ways)]
+
+    def mid_perm(shift):
+        return [
+            (i, (i // (2 * middle)) * 2 * middle + ((i // 2 + shift) % middle) * 2 + i % 2)
+            for i in range(seq_ways)
+        ]
+
+    def out_perm(shift):
+        return [(i, (i + shift * 2 * middle) % seq_ways) for i in range(seq_ways)]
+
+    def tok_perm(shift):
+        return [(i, (i + shift) % tok_ways) for i in range(tok_ways)]
+
+    rows, width = gradient.shape[0] // seq_ways, gradient.shape[1]
+    parts = gradient.astype(jnp.bfloat16).reshape(outer * middle, 2, rows, width)
+    parts = group_scatter(jnp.swapaxes(parts, 0, 1), core, 2, "seq", core_perm)
+    parts = parts.reshape(outer, middle, rows, 2, tok_ways, width // (2 * tok_ways))
+    first = jnp.transpose(parts[:, :, :, 0], (1, 3, 0, 2, 4))
+    second = jnp.transpose(parts[:, :, :, 1], (3, 1, 0, 2, 4))
+    first = group_scatter(first, mid, middle, "seq", mid_perm)
+    second = group_scatter(second, turn, tok_ways, "tok", tok_perm)
+    first = group_scatter(first, turn, tok_ways, "tok", tok_perm)
+    second = group_scatter(second, mid, middle, "seq", mid_perm)
+    both = jnp.stack([first, second], axis=1)
+    both = group_scatter(both, out, outer, "seq", out_perm)
+    both = group_gather(both, turn, tok_ways, "tok", tok_perm)
+    return jnp.transpose(both, (2, 1, 0, 3)).reshape(rows, width).T.astype(jnp.float32)
 
 
 def body(
@@ -140,11 +202,18 @@
     b_down,
     cotangent,
 ):
-    seq_count, sub_len, model_width = tokens.shape
-    tok_ways = lax.axis_size("tok")
-    row_count = seq_count * sub_len
-    embed_table = noise_table(noise_times).astype(jnp.bfloat16)
+    seq_ways, tok_ways = lax.axis_size("seq"), lax.axis_size("tok")
+    model_width = tokens.shape[-1]
+    seq_count, length = tokens.shape[0] // tok_ways, tokens.shape[1] * tok_ways
+    row_count = seq_count * length
+    all_times = lax.all_gather(noise_times, "seq", tiled=True)
+    own_times = lax.dynamic_slice_in_dim(
+        noise_times, lax.axis_index("tok") * seq_count, seq_count
+    )
+    embed_table = noise_table(own_times).astype(jnp.bfloat16)
     time_embed = product(embed_table, time_proj) + time_bias.astype(jnp.float32)
+    tokens = gather_sequences(tokens)
+    incoming = gather_sequences(cotangent).reshape(row_count, model_width)
     hidden_zero = (tokens.astype(jnp.float32) + time_embed[:, None, :]).reshape(
         row_count, model_width
     )
@@ -152,15 +221,11 @@
         layer_norm, hidden_zero, gain_one.astype(jnp.float32), shift_one.astype(jnp.float32)
     )
     normed_one = normed_one.astype(jnp.bfloat16)
-    projected = (
-        product(normed_one, w_qkv).astype(jnp.bfloat16).reshape(seq_count, sub_len, 3, tok_ways, -1)
-    )
+    projected = product(normed_one, w_qkv).astype(jnp.bfloat16)
     received, attended, log_total = attend_items(
-        lax.all_to_all(projected, "tok", split_axis=3, concat_axis=1, tiled=True)
-    )
-    attended = lax.all_to_all(attended, "tok", split_axis=1, concat_axis=2, tiled=True).reshape(
-        row_count, model_width
-    )
+        projected.reshape(seq_count, length, 3, 1, model_width)
+    )
+    attended = attended.reshape(row_count, model_width)
     hidden_one = hidden_zero + product(attended, w_out)
     normed_two, pull_two = jax.vjp(
         layer_norm, hidden_one, gain_two.astype(jnp.float32), shift_two.astype(jnp.float32)
@@ -169,124 +234,72 @@
     upward = product(normed_two, w_up) + b_up.astype(jnp.float32)
     active, pull_gelu = jax.vjp(jax.nn.gelu, upward)
     active = active.astype(jnp.bfloat16)
+    out_wdown = scatter_sum(contract_rows(incoming, active))
     result = hidden_one + (product(active, w_down) + b_down.astype(jnp.float32))
-    incoming = cotangent.reshape(row_count, model_width)
+    mixed_out = return_positions(
+        result.astype(jnp.bfloat16).reshape(seq_count, length, model_width)
+    )
     sum_down = jnp.sum(incoming, axis=0, dtype=jnp.float32)
-    grad_w_down = contract_rows(active, incoming)
     grad_active = times_transpose(incoming, w_down)
     (grad_upward,) = pull_gelu(grad_active)
     grad_upward = grad_upward.astype(jnp.bfloat16)
     sum_up = jnp.sum(grad_upward, axis=0, dtype=jnp.float32)
-    grad_w_up = contract_rows(normed_two, grad_upward)
+    out_wup = scatter_sum(contract_rows(grad_upward, normed_two))
     grad_norm_two = times_transpose(grad_upward, w_up)
     grad_hidden_two, grad_gain_two, grad_shift_two = pull_two(grad_norm_two)
     grad_hidden_one = incoming.astype(jnp.float32) + grad_hidden_two
     grad_attn = grad_hidden_one.astype(jnp.bfloat16)
-    grad_w_out = contract_rows(attended, grad_attn)
-    grad_mixed = (
-        times_transpose(grad_attn, w_out)
-        .astype(jnp.bfloat16)
-        .reshape(seq_count, sub_len, tok_ways, -1)
-    )
-    grad_heads = lax.all_to_all(grad_mixed, "tok", split_axis=2, concat_axis=1, tiled=True)
-    grad_parts = attention_grad(received, log_total, grad_heads)
-    grad_parts = lax.all_to_all(grad_parts, "tok", split_axis=1, concat_axis=3, tiled=True).reshape(
-        row_count, 3 * model_width
-    )
-    grad_w_qkv = contract_rows(normed_one, grad_parts)
+    out_wout = scatter_sum(contract_rows(grad_attn, attended))
+    grad_mixed = times_transpose(grad_attn, w_out).astype(jnp.bfloat16)
+    grad_parts = attention_grad(
+        received, log_total, grad_mixed.reshape(seq_count, length, 1, model_width)
+    ).reshape(row_count, 3 * model_width)
+    out_wqkv = scatter_sum(contract_rows(grad_parts, normed_one))
     grad_norm_one = times_transpose(grad_parts, w_qkv)
     grad_hidden_zero, grad_gain_one, grad_shift_one = pull_one(grad_norm_one)
     grad_total = grad_hidden_one + grad_hidden_zero
-    grad_tokens = grad_total.astype(jnp.bfloat16).reshape(seq_count, sub_len, model_width)
-    grad_embed = jnp.sum(grad_total.reshape(seq_count, sub_len, model_width), axis=1)
-    grad_time_bias = jnp.sum(grad_embed, axis=0)
-    grad_time_proj = jnp.dot(
-        embed_table.astype(jnp.float32).T, grad_embed, precision=lax.Precision.HIGHEST
-    )
-    summed = (
-        lax.psum_scatter(
-            grad_time_proj.astype(jnp.bfloat16), "seq", scatter_dimension=1, tiled=True
-        ).astype(jnp.float32),
-        lax.psum_scatter(
-            grad_time_bias[None, :].astype(jnp.bfloat16), "seq", scatter_dimension=1, tiled=True
-        ).astype(jnp.float32),
-        lax.psum_scatter(
-            grad_gain_one[None, :].astype(jnp.bfloat16), "seq", scatter_dimension=1, tiled=True
-        ).astype(jnp.float32),
-        lax.psum_scatter(
-            grad_shift_one[None, :].astype(jnp.bfloat16), "seq", scatter_dimension=1, tiled=True
-        ).astype(jnp.float32),
-        lax.psum_scatter(
-            grad_w_qkv.astype(jnp.bfloat16), "seq", scatter_dimension=1, tiled=True
-        ).astype(jnp.float32),
-        lax.psum_scatter(
-            grad_w_out.astype(jnp.bfloat16), "seq", scatter_dimension=1, tiled=True
-        ).astype(jnp.float32),
-        lax.psum_scatter(
-            grad_gain_two[None, :].astype(jnp.bfloat16), "seq", scatter_dimension=1, tiled=True
-        ).astype(jnp.float32),
-        lax.psum_scatter(
-            grad_shift_two[None, :].astype(jnp.bfloat16), "seq", scatter_dimension=1, tiled=True
-        ).astype(jnp.float32),
-        lax.psum_scatter(
-            grad_w_up.astype(jnp.bfloat16), "seq", scatter_dimension=1, tiled=True
-        ).astype(jnp.float32),
-        lax.psum_scatter(
-            sum_up[None, :].astype(jnp.bfloat16), "seq", scatter_dimension=1, tiled=True
-        ).astype(jnp.float32),
-        lax.psum_scatter(
-            grad_w_down.astype(jnp.bfloat16), "seq", scatter_dimension=1, tiled=True
-        ).astype(jnp.float32),
-        lax.psum_scatter(
-            sum_down[None, :].astype(jnp.bfloat16), "seq", scatter_dimension=1, tiled=True
-        ).astype(jnp.float32),
-    )
-    summed = (
-        lax.psum(summed[0].astype(jnp.bfloat16), "tok").astype(jnp.float32),
-        lax.psum(summed[1].astype(jnp.bfloat16), "tok").astype(jnp.float32),
-        lax.psum(summed[2].astype(jnp.bfloat16), "tok").astype(jnp.float32),
-        lax.psum(summed[3].astype(jnp.bfloat16), "tok").astype(jnp.float32),
-        lax.psum(summed[4].astype(jnp.bfloat16), "tok").astype(jnp.float32),
-        lax.psum(summed[5].astype(jnp.bfloat16), "tok").astype(jnp.float32),
-        lax.psum(summed[6].astype(jnp.bfloat16), "tok").astype(jnp.float32),
-        lax.psum(summed[7].astype(jnp.bfloat16), "tok").astype(jnp.float32),
-        lax.psum(summed[8].astype(jnp.bfloat16), "tok").astype(jnp.float32),
-        lax.psum(summed[9].astype(jnp.bfloat16), "tok").astype(jnp.float32),
-        lax.psum(summed[10].astype(jnp.bfloat16), "tok").astype(jnp.float32),
-        lax.psum(summed[11].astype(jnp.bfloat16), "tok").astype(jnp.float32),
-    )
-    out_proj, out_wqkv, out_wout, out_wup, out_wdown = (
-        summed[0],
-        summed[4],
-        summed[5],
-        summed[8],
-        summed[10],
-    )
-    out_vectors = (
-        summed[1][0],
-        summed[2][0],
-        summed[3][0],
-        summed[6][0],
-        summed[7][0],
-        summed[9][0],
-        summed[11][0],
-    )
-    mixed_out = result.astype(jnp.bfloat16).reshape(seq_count, sub_len, model_width)
+    grad_tokens = return_positions(
+        grad_total.astype(jnp.bfloat16).reshape(seq_count, length, model_width)
+    )
+    grad_embed = jnp.sum(grad_total.reshape(seq_count, length, model_width), axis=1)
+    wide = sum_up.shape[0] // model_width
+    small = jnp.concatenate(
+        [
+            grad_embed.reshape(seq_count, seq_ways, -1).swapaxes(0, 1),
+            grad_gain_one.reshape(seq_ways, 1, -1),
+            grad_shift_one.reshape(seq_ways, 1, -1),
+            grad_gain_two.reshape(seq_ways, 1, -1),
+            grad_shift_two.reshape(seq_ways, 1, -1),
+            sum_down.reshape(seq_ways, 1, -1),
+            sum_up.reshape(seq_ways, wide, -1),
+        ],
+        axis=1,
+    )
+    small = lax.all_to_all(small, "seq", split_axis=0, concat_axis=0, tiled=True)
+    small = lax.all_gather(small, "tok", axis=1)
+    embeds = small[:, :, :seq_count].reshape(-1, small.shape[-1])
+    out_proj = jnp.dot(
+        noise_table(all_times).astype(jnp.bfloat16).astype(jnp.float32).T,
+        embeds,
+        precision=lax.Precision.HIGHEST,
+    )
+    out_bias = jnp.sum(embeds, axis=0)
+    sums = jnp.sum(small[:, :, seq_count:], axis=(0, 1))
     return (
         mixed_out,
         grad_tokens,
         out_proj,
-        out_vectors[0],
-        out_vectors[1],
-        out_vectors[2],
+        out_bias,
+        sums[0],
+        sums[1],
         out_wqkv,
         out_wout,
-        out_vectors[3],
-        out_vectors[4],
+        sums[2],
+        sums[3],
         out_wup,
-        out_vectors[5],
+        sums[5:].reshape(-1),
         out_wdown,
-        out_vectors[6],
+        sums[4],
     )
 
 

time: 1090 us -> 509 us (0.47)
  waiting for transfers between devices: 746 us -> 62.9 us
  local copies, waits for them, and re-layouts: 95.8 us -> 167 us
  starting transfers between devices: 14.7 us -> 62.5 us
  other arithmetic: 57.8 us -> 84.9 us
  blocking collectives: 46.3 us -> 28.2 us
  matrix products: 109 us -> 93 us
  between operations: 14.8 us -> 3.23 us
    unnamed x20 -> x0, waiting for transfers between devices: 334 us -> none
    reduce_scatter x5 -> x0, waiting for transfers between devices: 316 us -> none  [the longest x1 109 us: body(): lax.psum_scatter(grad_w_up.astype(jnp.bfloat16), 'seq', scatter_dimension...]
    ppermute x0 -> x36, waiting for transfers between devices: none -> 58.7 us  [the longest x32 48.4 us: group_scatter(): lax.ppermute(piece, axis, perm_of(shift)).astype(jnp.float32)]
    all_to_all x3 -> x5, waiting for transfers between devices: 56.5 us -> 4.21 us  [the longest x2 4.2 us: return_positions(): lax.all_to_all(values, 'tok', split_axis=1, concat_axis=0, tiled=True)]
    ppermute x0 -> x36, starting transfers between devices: none -> 42 us  [the longest x32 37.2 us: group_scatter(): lax.ppermute(piece, axis, perm_of(shift)).astype(jnp.float32)]
    psum x1 -> x0, waiting for transfers between devices: 40.1 us -> none  [body(): lax.psum(summed[4].astype(jnp.bfloat16), 'tok').astype(jnp.float32)]
    all_to_all x1 -> x0, blocking collectives: 37.1 us -> none  [body(): lax.all_to_all(grad_parts, 'tok', split_axis=1, concat_axis=3, tiled=True)]
    dynamic_update_slice x0 -> x7, local copies, waits for them, and re-layouts: none -> 32.2 us  [the longest x4 16.2 us: group_gather(): held = lax.dynamic_update_index_in_dim(held, other, (own - shift) % size, 0)]
  transfers between devices with their start and end apart: 16 -> 41, of which waited for: 14 -> 11; matrix products, arithmetic and copies ran while one was open for 15% -> 43% of each run, Pallas kernels for 0% -> 0%
where the time goes in v1:
time: 509 us; the launch traced here: 502 us
  local copies, waits for them, and re-layouts  167 us (33%)
  matrix products  93 us (18%)
  other arithmetic  84.9 us (17%)
  waiting for transfers between devices  62.9 us (12%)
  starting transfers between devices  62.5 us (12%)
  blocking collectives  28.2 us (6%)
    ppermute x32, waiting for transfers between devices, group_scatter(): lax.ppermute(piece, axis, perm_of(shift)).astype(jnp.float32)  48.4 us
    ppermute x32, starting transfers between devices, group_scatter(): lax.ppermute(piece, axis, perm_of(shift)).astype(jnp.float32)  37.2 us
    convert_element_type x15, other arithmetic, group_scatter(): return total.astype(jnp.bfloat16)  35.2 us
    unnamed x153, local copies, waits for them, and re-layouts  33.1 us
    dot_general x5, matrix products, product(): return jnp.dot(left_side, right_side, preferred_element_type=jnp.float32)  30 us
    dot_general x4, matrix products, contract_rows(): jnp.einsum('ra,rb->ab', left_side, right_side, preferred_element_type=jnp...  27.3 us
    dot_general x4, matrix products, times_transpose(): jnp.einsum('rb,ab->ra', left_side, right_side, preferred_element_type=jnp...  25.4 us
    reshape x4, local copies, waits for them, and re-layouts, scatter_sum(): parts.reshape(outer, middle, rows, 2, tok_ways, width // (2 * tok_ways))  23.6 us
  transfers between devices with their start and end apart: 41, of which 11 were waited for; matrix products, arithmetic and copies ran while one was open for 43% of the time, Pallas kernels for 0%

profile of v1, /device:TPU:0, one launch (start us, length us, event | category | flops | bytes accessed | tf_op | source)
XLA Modules:
  0.0 501.6 jit_solution(4558560201841461523)
XLA Ops:
  7.1 13.1 %all-reduce = s32[128]{0:T(128)S(1)} all-reduce(s32[128]{0:T(128)S(1)} %dynamic-update-slice), channel_id=1, replica_groups=mesh['seq'=16,'tok'=2] {'seq'}, use_global_device_ids=true, to_apply=%add | all-reduce | flops 128 | bytes 1024
  22.6 4.5 all-to-all-start.2
  32.4 7.9 %convolution_convert_fusion.3 = bf16[512,3072]{1,0:T(8,128)(2,1)} fusion(bf16[512,1024]{1,0:T(8,128)(2,1)S(1)} %add_convert_fusion.2, bf16[1024,3072]{1,0:T(8,128)(2,1)} %param.21), kind=kOutput, calls=%fused_computation.21 | convolution fusion | flops 3222798336 | bytes 10485760 | tf_op jit(solution)/shard_map/dot_general | solution.py:47
  40.2 4.6 copy.238
  44.9 5.5 %reshape_reshape.11 = bf16[4,128,3,16,64]{1,0,4,3,2:T(4,128)(2,1)} reshape(bf16[512,3072]{0,1:T(8,128)(2,1)} %copy.238) | data formatting | bytes 6291456 | tf_op jit(solution)/shard_map/reshape;reshape | solution.py:61
  68.2 10.5 %fusion.149 = f32[512,4096]{1,0:T(8,128)} fusion(bf16[1024,4096]{1,0:T(8,128)(2,1)} %param.25, f32[512,1024]{1,0:T(8,128)S(1)} %copy-done.10, f32[1024]{0:T(1024)S(1)} %convert_element_type.608, f32[1024]{0:T(1024)S(1)} %convert_element_type.607, f32[512]{0:T(512)S(1)} %fusion.142, f32[512]{0:T(512)S(1)} %broadcast_multiply_fusion.3), kind=kOutput, calls=%fused_computation.326 | convolution fusion | flops 4297588736 | bytes 18886656 | tf_op jit(solution)/shard_map/dot_general | solution.py:47
  78.7 13.9 %convert_reduce_fusion = (f32[4096]{0:T(1024)S(1)}, bf16[512,4096]{1,0:T(8,128)(2,1)S(1)}) fusion(f32[512,4096]{1,0:T(8,128)} %fusion.149, f32[4096]{0:T(1024)S(1)} %convert_element_type.610, bf16[512,1024]{1,0:T(8,128)(2,1)S(1)} %bitcast.476, bf16[4096,1024]{1,0:T(8,128)(2,1)} %param.27), kind=kOutput, calls=%fused_computation.13 | convolution fusion | flops 4343197696 | bytes 22052864 | tf_op jit(solution)/shard_map/rb,ab->ra/dot_general | solution.py:55
  92.6 5.0 multiply_reduce_fusion.2
  137.8 7.6 %convolution_convert_fusion.1 = bf16[4096,1024]{1,0:T(8,128)(2,1)} fusion(bf16[512,4096]{1,0:T(8,128)(2,1)S(1)} %copy-done.55, f32[512,1024]{1,0:T(8,128)S(1)} %copy-done.11, f32[1024]{0:T(1024)S(1)} %convert_element_type.608, f32[1024]{0:T(1024)S(1)} %convert_element_type.607, f32[512]{0:T(512)S(1)} %fusion.142, f32[512]{0:T(512)S(1)} %broadcast_multiply_fusion.3), kind=kOutput, calls=%fused_computation.16 | convolution fusion | flops 4301783040 | bytes 14692352 | tf_op jit(solution)/shard_map/ra,rb->ab/dot_general | solution.py:51
  145.4 11.7 %convolution_convert_fusion = bf16[4096,1024]{0,1:T(8,128)(2,1)} fusion(bf16[512,1024]{1,0:T(8,128)(2,1)S(1)} %bitcast.477, f32[512,4096]{1,0:T(8,128)} %fusion.149, f32[4096]{0:T(1024)S(1)} %convert_element_type.610), kind=kOutput, calls=%fused_computation.15 | convolution fusion | flops 4320133120 | bytes 17842176 | tf_op jit(solution)/shard_map/ra,rb->ab/dot_general | solution.py:51
  157.1 9.0 %add_convert_fusion = bf16[512,1024]{1,0:T(8,128)(2,1)S(1)} fusion(f32[512,1024]{1,0:T(8,128)S(1)} %copy-done.11, bf16[4096,1024]{1,0:T(8,128)(2,1)S(1)} %bitcast.523, f32[1024]{0:T(1024)S(1)} %convert_element_type.612, f32[512,4096]{1,0:T(8,128)} %fusion.149, f32[4096]{0:T(1024)S(1)} %convert_element_type.610), kind=kOutput, calls=%fused_computation.89 | convolution fusion | flops 4317511680 | bytes 19943424 | tf_op jit(solution)/shard_map/dot_general | solution.py:47
  196.8 15.1 %all-gather = f32[16,26,64]{2,0,1:T(8,128)S(1)} all-gather(f32[16,13,64]{2,0,1:T(8,128)S(1)} %copy.260), channel_id=2, replica_groups=mesh['seq'=16,'tok'=2] {'tok'}, dimensions={1}, use_global_device_ids=true | all-gather | bytes 159744 | tf_op jit(solution)/shard_map/all_gather | solution.py:279
  222.3 4.5 collective-permute-done.12
  235.3 6.3 %fusion.9 = bf16[8,192,1024]{2,1,0:T(8,128)(2,1)} fusion(bf16[8,192,1024]{2,1,0:T(8,128)(2,1)} %collective-permute-done, bf16[8,2,192,1024]{3,2,1,0:T(8,128)(2,1)} %bitcast.491, s32[]{:T(128)S(6)} %select_n.233), kind=kLoop, calls=%fused_computation.19 | loop fusion | flops 6291456 | bytes 9437188 | tf_op jit(solution)/shard_map/convert_element_type | solution.py:139
  241.6 6.1 %reshape.525 = bf16[4,2,192,2,2,256]{5,4,3,2,1,0:T(2,128)(2,1)} reshape(bf16[8,192,1024]{2,1,0:T(8,128)(2,1)} %fusion.9) | data formatting | bytes 6291456 | tf_op jit(solution)/shard_map/reshape | solution.py:175
  283.1 10.2 %collective-permute-done.17 = bf16[2,64,256]{2,1,0:T(8,128)(2,1)S(1)} collective-permute-done((bf16[2,64,256]{2,1,0:T(8,128)(2,1)S(1)}, bf16[2,64,256]{2,1,0:T(8,128)(2,1)S(1)}, u32[]{:S(2)}, u32[]{:S(2)}) %collective-permute-start.17) | collective-permute-done | bytes 65568 | tf_op jit(solution)/shard_map/ppermute | solution.py:146
  304.4 7.8 %fusion.8 = bf16[8,256,1024]{2,1,0:T(8,128)(2,1)} fusion(bf16[8,256,1024]{2,1,0:T(8,128)(2,1)} %collective-permute-done.18, bf16[8,2,256,1024]{3,2,1,0:T(8,128)(2,1)} %bitcast.484, s32[]{:T(128)S(6)} %select_n.233), kind=kLoop, calls=%fused_computation.12 | loop fusion | flops 8388608 | bytes 12582916 | tf_op jit(solution)/shard_map/convert_element_type | solution.py:139
  312.1 7.8 %reshape.533 = bf16[4,2,256,2,2,256]{5,4,3,2,1,0:T(2,128)(2,1)} reshape(bf16[8,256,1024]{2,1,0:T(8,128)(2,1)} %fusion.8) | data formatting | bytes 8388608 | tf_op jit(solution)/shard_map/reshape | solution.py:175
  319.9 4.7 fusion.155
  332.5 6.8 %constant_dynamic-slice_fusion.3 = (bf16[4,2,256,1,1,256]{5,4,3,2,1,0:T(2,128)(2,1)}, bf16[4,2,256,1,1,256]{5,4,3,2,1,0:T(2,128)(2,1)}) fusion(bf16[4,2,256,1,2,256]{5,4,3,2,1,0:T(2,128)(2,1)S(1)} %get-tuple-element.30, s32[]{:T(128)S(6)} %select_n.241, s32[]{:T(128)S(6)} %select_n.243), kind=kLoop, calls=%fused_computation.280 | loop fusion | bytes 4194312 | tf_op jit(solution)/shard_map/dynamic-slice.34
  339.3 5.8 %copy.303 = bf16[4,2,256,1,1,256]{2,5,0,1,4,3:T(8,128)(2,1)} copy(bf16[4,2,256,1,1,256]{5,4,3,2,1,0:T(2,128)(2,1)} %get-tuple-element.42) | data formatting | bytes 2097152
  346.8 7.3 %fusion.7 = bf16[8,64,4096]{2,1,0:T(8,128)(2,1)} fusion(bf16[8,64,4096]{2,1,0:T(8,128)(2,1)} %collective-permute-done.27, bf16[8,2,64,4096]{3,2,1,0:T(8,128)(2,1)} %bitcast.480, s32[]{:T(128)S(6)} %select_n.233), kind=kLoop, calls=%fused_computation.10 | loop fusion | flops 8388608 | bytes 12582916 | tf_op jit(solution)/shard_map/convert_element_type | solution.py:139
  354.2 7.8 %reshape.538 = bf16[4,2,64,2,2,1024]{5,4,3,2,1,0:T(2,128)(2,1)} reshape(bf16[8,64,4096]{2,1,0:T(8,128)(2,1)} %fusion.7) | data formatting | bytes 8388608 | tf_op jit(solution)/shard_map/reshape | solution.py:175
  362.0 5.8 %fusion.154 = (bf16[4,2,64,1,2,1024]{5,4,3,2,1,0:T(2,128)(2,1)S(1)}, bf16[4,2,64,1,2,1024]{5,4,3,2,1,0:T(2,128)(2,1)}) fusion(bf16[4,2,64,2,2,1024]{5,4,3,2,1,0:T(2,128)(2,1)} %reshape.538), kind=kLoop, calls=%fused_computation.329 | loop fusion | bytes 8388608 | tf_op jit(solution)/shard_map/slice | solution.py:177
  377.2 6.9 %constant_dynamic-slice_fusion = (bf16[4,2,64,1,1,1024]{5,4,3,2,1,0:T(2,128)(2,1)}, f32[1,2,4,64,1024]{4,0,3,1,2:T(1,128)}) fusion(bf16[4,2,64,1,2,1024]{5,4,3,2,1,0:T(2,128)(2,1)S(1)} %get-tuple-element.28, s32[]{:T(128)S(6)} %select_n.243, s32[]{:T(128)S(6)} %select_n.241), kind=kLoop, calls=%fused_computation.277 | loop fusion | flops 524288 | bytes 5242888 | tf_op jit(solution)/shard_map/dynamic-slice.39
  399.1 17.2 %collective-permute-done.28 = bf16[2,4,64,1024]{3,0,2,1:T(2,128)(2,1)S(1)} collective-permute-done((bf16[2,4,64,1024]{3,0,2,1:T(2,128)(2,1)S(1)}, bf16[2,4,64,1024]{3,0,2,1:T(2,128)(2,1)S(1)}, u32[]{:S(2)}, u32[]{:S(2)}) %collective-permute-start.28) | collective-permute-done | bytes 1048608 | tf_op jit(solution)/shard_map/ppermute | solution.py:138
  421.4 9.5 %collective-permute-done.20 = bf16[4,256,256]{1,2,0:T(8,128)(2,1)S(1)} collective-permute-done((bf16[4,256,256]{1,2,0:T(8,128)(2,1)S(1)}, bf16[4,256,256]{1,2,0:T(8,128)(2,1)S(1)}, u32[]{:S(2)}, u32[]{:S(2)}) %collective-permute-start.20) | collective-permute-done | bytes 524320 | tf_op jit(solution)/shard_map/ppermute | solution.py:138
  446.7 5.0 dynamic_update_slice.28
  453.0 5.0 dynamic_update_slice.29
  458.0 7.4 %collective-permute-done.24 = bf16[2,256,256]{1,2,0:T(8,128)(2,1)S(1)} collective-permute-done((bf16[2,256,256]{1,2,0:T(8,128)(2,1)}, bf16[2,256,256]{1,2,0:T(8,128)(2,1)S(1)}, u32[]{:S(2)}, u32[]{:S(2)}) %collective-permute-start.24) | collective-permute-done | bytes 262176 | tf_op jit(solution)/shard_map/ppermute | solution.py:138
  477.6 9.3 %dynamic_update_slice.34 = bf16[2,2,64,1024]{3,0,1,2:T(2,128)(2,1)} dynamic-update-slice(bf16[2,2,64,1024]{3,0,1,2:T(2,128)(2,1)} %broadcast_in_dim.102, bf16[1,2,64,1024]{3,0,1,2:T(2,128)(2,1)S(1)} %copy.275, s32[]{:T(128)S(6)} %select_n.241, s32[]{:T(128)} %constant.376.clone.1, s32[]{:T(128)} %constant.376.clone.1, s32[]{:T(128)} %constant.376.clone.1) | dynamic-update-slice | bytes 524292 | tf_op jit(solution)/shard_map/jit(dynamic_update_index_in_dim)/dynamic_update_slice | solution.py:144
  488.4 9.5 %dynamic_update_slice.35 = bf16[2,2,64,1024]{3,0,1,2:T(2,128)(2,1)} dynamic-update-slice(bf16[2,2,64,1024]{3,0,1,2:T(2,128)(2,1)} %dynamic_update_slice.34, bf16[1,2,64,1024]{3,0,1,2:T(2,128)(2,1)S(1)} %copy.276, s32[]{:T(128)S(6)} %select_n.253, s32[]{:T(128)} %constant.376.clone.1, s32[]{:T(128)} %constant.376.clone.1, s32[]{:T(128)} %constant.376.clone.1) | dynamic-update-slice | bytes 524292 | tf_op jit(solution)/shard_map/jit(dynamic_update_index_in_dim)/dynamic_update_slice | solution.py:147
  (393 shorter events, 239.3 us)
Async XLA Ops:
  0.8 21.8 %all-to-all-start = ((bf16[8,64,1024]{2,1,0:T(8,128)(2,1)}), bf16[8,64,1024]{2,1,0:T(8,128)(2,1)S(1)}, u32[]{:S(2)}, u32[]{:S(2)}) async-start(bf16[8,64,1024]{2,1,0:T(8,128)(2,1)} %param.15), calls=%async_computation | async-start | bytes 2097152 | tf_op jit(solution)/shard_map/all_to_all | solution.py:127
  22.6 43.6 %all-to-all-start.2 = ((bf16[8,64,1024]{2,1,0:T(8,128)(2,1)}), bf16[8,64,1024]{2,1,0:T(8,128)(2,1)}, u32[]{:S(2)}, u32[]{:S(2)}) async-start(bf16[8,64,1024]{2,1,0:T(8,128)(2,1)} %param.29), calls=%async_computation.2 | async-start | bytes 2097152 | tf_op jit(solution)/shard_map/all_to_all | solution.py:127
  171.1 20.6 %all-to-all-start.4 = ((f32[16,1,832]{2,1,0:T(1,128)}), f32[16,1,832]{2,1,0:T(1,128)S(1)}, u32[]{:S(2)}, u32[]{:S(2)}) async-start(f32[16,1,832]{2,1,0:T(1,128)} %reshape.591), calls=%async_computation.4 | async-start | bytes 114688 | tf_op jit(solution)/shard_map/all_to_all | solution.py:278
  181.5 30.9 %collective-permute-start.9 = (bf16[8,64,1024]{2,1,0:T(8,128)(2,1)}, bf16[8,64,1024]{2,1,0:T(8,128)(2,1)}, u32[]{:S(2)}, u32[]{:S(2)}) collective-permute-start(bf16[8,64,1024]{2,1,0:T(8,128)(2,1)} %dynamic-slice_bitcast_fusion.4), channel_id=1, source_target_pairs={{0,2},{2,0},{4,6},{6,4},{8,10},{10,8},{12,14},{14,12},{16,18},{18,... | collective-permute-start | bytes 3145736 | tf_op jit(solution)/shard_map/ppermute | solution.py:138
  185.4 50.0 %collective-permute-start = (bf16[8,192,1024]{2,1,0:T(8,128)(2,1)}, bf16[8,192,1024]{2,1,0:T(8,128)(2,1)}, u32[]{:S(2)}, u32[]{:S(2)}) collective-permute-start(bf16[8,192,1024]{2,1,0:T(8,128)(2,1)} %dynamic-slice_bitcast_fusion.2), channel_id=1, source_target_pairs={{0,2},{2,0},{4,6},{6,4},{8,10},{10,8},{12,14},{14,12},{16,18},{18,... | collective-permute-start | bytes 9437192 | tf_op jit(solution)/shard_map/ppermute | solution.py:138
  188.2 116.2 %collective-permute-start.18 = (bf16[8,256,1024]{2,1,0:T(8,128)(2,1)}, bf16[8,256,1024]{2,1,0:T(8,128)(2,1)}, u32[]{:S(2)}, u32[]{:S(2)}) collective-permute-start(bf16[8,256,1024]{2,1,0:T(8,128)(2,1)} %dynamic-slice_bitcast_fusion.1), channel_id=1, source_target_pairs={{0,2},{2,0},{4,6},{6,4},{8,10},{10,8},{12,14},{14,12},{16,18},{18,... | collective-permute-start | bytes 12582920 | tf_op jit(solution)/shard_map/ppermute | solution.py:138
  190.7 156.1 %collective-permute-start.27 = (bf16[8,64,4096]{2,1,0:T(8,128)(2,1)}, bf16[8,64,4096]{2,1,0:T(8,128)(2,1)}, u32[]{:S(2)}, u32[]{:S(2)}) collective-permute-start(bf16[8,64,4096]{2,1,0:T(8,128)(2,1)} %dynamic-slice_bitcast_fusion), channel_id=1, source_target_pairs={{0,2},{2,0},{4,6},{6,4},{8,10},{10,8},{12,14},{14,12},{16,18},{18,... | collective-permute-start | bytes 12582920 | tf_op jit(solution)/shard_map/ppermute | solution.py:138
  191.8 67.3 %all-to-all-start.1 = ((bf16[4,128,1024]{2,0,1:T(4,128)(2,1)}), bf16[4,128,1024]{2,0,1:T(4,128)(2,1)S(1)}, u32[]{:S(2)}, u32[]{:S(2)}) async-start(bf16[4,128,1024]{2,0,1:T(4,128)(2,1)} %copy.244), calls=%async_computation.1 | async-start | bytes 2097152 | tf_op jit(solution)/shard_map/all_to_all | solution.py:131
  254.2 41.5 %collective-permute-start.1 = (bf16[2,4,192,256]{3,0,2,1:T(2,128)(2,1)}, bf16[2,4,192,256]{3,0,2,1:T(2,128)(2,1)}, u32[]{:S(2)}, u32[]{:S(2)}) collective-permute-start(bf16[2,4,192,256]{3,0,2,1:T(2,128)(2,1)} %dynamic-slice_bitcast_fusion.5), channel_id=1, source_target_pairs={{0,4},{2,6},{4,0},{6,2},{8,12},{10,14},{12,8},{14,10},{16,20},{18,... | collective-permute-start | bytes 2359304 | tf_op jit(solution)/shard_map/ppermute | solution.py:138
  259.0 19.6 %all-to-all-start.3 = ((bf16[4,128,1024]{2,0,1:T(4,128)(2,1)}), bf16[4,128,1024]{2,0,1:T(4,128)(2,1)}, u32[]{:S(2)}, u32[]{:S(2)}) async-start(bf16[4,128,1024]{2,0,1:T(4,128)(2,1)} %copy.256), calls=%async_computation.3 | async-start | bytes 2097152 | tf_op jit(solution)/shard_map/all_to_all | solution.py:131
  269.9 31.6 %collective-permute-start.3 = (bf16[2,4,192,256]{3,2,0,1:T(8,128)(2,1)}, bf16[2,4,192,256]{3,2,0,1:T(8,128)(2,1)}, u32[]{:S(2)}, u32[]{:S(2)}) collective-permute-start(bf16[2,4,192,256]{3,2,0,1:T(8,128)(2,1)} %bitcast.469), channel_id=1, source_target_pairs={{0,1},{1,0},{2,3},{3,2},{4,5},{5,4},{6,7},{7,6},{8,9},{9,8},{10,11... | collective-permute-start | bytes 2359304 | tf_op jit(solution)/shard_map/ppermute | solution.py:138
  271.9 21.4 %collective-permute-start.17 = (bf16[2,64,256]{2,1,0:T(8,128)(2,1)S(1)}, bf16[2,64,256]{2,1,0:T(8,128)(2,1)S(1)}, u32[]{:S(2)}, u32[]{:S(2)}) collective-permute-start(bf16[2,64,256]{2,1,0:T(8,128)(2,1)S(1)} %fusion.120), channel_id=1, source_target_pairs={{0,1},{1,0},{2,3},{3,2},{4,5},{5,4},{6,7},{7,6},{8,9},{9,8},{10,11... | collective-permute-start | bytes 196616 | tf_op jit(solution)/shard_map/ppermute | solution.py:146
  301.1 66.6 %collective-permute-start.2 = (bf16[4,192,256]{2,1,0:T(8,128)(2,1)}, bf16[4,192,256]{2,1,0:T(8,128)(2,1)S(1)}, u32[]{:S(2)}, u32[]{:S(2)}) collective-permute-start(bf16[4,192,256]{2,1,0:T(8,128)(2,1)} %bitcast.471), channel_id=1, source_target_pairs={{0,1},{1,0},{2,3},{3,2},{4,5},{5,4},{6,7},{7,6},{8,9},{9,8},{10,11... | collective-permute-start | bytes 1179656 | tf_op jit(solution)/shard_map/ppermute | solution.py:138
  303.7 65.9 %collective-permute-start.4 = (bf16[4,192,256]{2,1,0:T(8,128)(2,1)}, bf16[4,192,256]{2,1,0:T(8,128)(2,1)}, u32[]{:S(2)}, u32[]{:S(2)}) collective-permute-start(bf16[4,192,256]{2,1,0:T(8,128)(2,1)} %dynamic-slice_bitcast_fusion.9), channel_id=1, source_target_pairs={{0,4},{2,6},{4,0},{6,2},{8,12},{10,14},{12,8},{14,10},{16,20},{18,... | collective-permute-start | bytes 1179656 | tf_op jit(solution)/shard_map/ppermute | solution.py:138
  331.0 63.2 %collective-permute-start.19 = (bf16[2,4,256,256]{2,3,1,0:T(8,128)(2,1)}, bf16[2,4,256,256]{2,3,1,0:T(8,128)(2,1)}, u32[]{:S(2)}, u32[]{:S(2)}) collective-permute-start(bf16[2,4,256,256]{2,3,1,0:T(8,128)(2,1)} %bitcast.503), channel_id=1, source_target_pairs={{0,4},{2,6},{4,0},{6,2},{8,12},{10,14},{12,8},{14,10},{16,20},{18,... | collective-permute-start | bytes 3145736 | tf_op jit(solution)/shard_map/ppermute | solution.py:138
  345.1 51.0 %collective-permute-start.21 = (bf16[2,4,256,256]{2,3,1,0:T(8,128)(2,1)}, bf16[2,4,256,256]{2,3,1,0:T(8,128)(2,1)}, u32[]{:S(2)}, u32[]{:S(2)}) collective-permute-start(bf16[2,4,256,256]{2,3,1,0:T(8,128)(2,1)} %bitcast.108), channel_id=1, source_target_pairs={{0,1},{1,0},{2,3},{3,2},{4,5},{5,4},{6,7},{7,6},{8,9},{9,8},{10,11... | collective-permute-start | bytes 3145736 | tf_op jit(solution)/shard_map/ppermute | solution.py:138
  372.4 17.8 %collective-permute-start.7 = (bf16[2,192,256]{2,1,0:T(8,128)(2,1)}, bf16[2,192,256]{2,1,0:T(8,128)(2,1)}, u32[]{:S(2)}, u32[]{:S(2)}) collective-permute-start(bf16[2,192,256]{2,1,0:T(8,128)(2,1)} %get-tuple-element.67), channel_id=1, source_target_pairs={{0,24},{2,26},{4,28},{6,30},{8,0},{10,2},{12,4},{14,6},{16,8},{18,... | collective-permute-start | bytes 589832 | tf_op jit(solution)/shard_map/ppermute | solution.py:138
  373.1 17.8 %collective-permute-start.6 = (bf16[2,192,256]{2,1,0:T(8,128)(2,1)}, bf16[2,192,256]{2,1,0:T(8,128)(2,1)}, u32[]{:S(2)}, u32[]{:S(2)}) collective-permute-start(bf16[2,192,256]{2,1,0:T(8,128)(2,1)} %get-tuple-element.66), channel_id=1, source_target_pairs={{0,16},{2,18},{4,20},{6,22},{8,24},{10,26},{12,28},{14,30},{16,0},... | collective-permute-start | bytes 589832 | tf_op jit(solution)/shard_map/ppermute | solution.py:138
  375.0 16.2 %collective-permute-start.5 = (bf16[2,192,256]{2,1,0:T(8,128)(2,1)}, bf16[2,192,256]{2,1,0:T(8,128)(2,1)}, u32[]{:S(2)}, u32[]{:S(2)}) collective-permute-start(bf16[2,192,256]{2,1,0:T(8,128)(2,1)} %get-tuple-element.65), channel_id=1, source_target_pairs={{0,8},{2,10},{4,12},{6,14},{8,16},{10,18},{12,20},{14,22},{16,24},... | collective-permute-start | bytes 589832 | tf_op jit(solution)/shard_map/ppermute | solution.py:138
  390.2 26.2 %collective-permute-start.28 = (bf16[2,4,64,1024]{3,0,2,1:T(2,128)(2,1)S(1)}, bf16[2,4,64,1024]{3,0,2,1:T(2,128)(2,1)S(1)}, u32[]{:S(2)}, u32[]{:S(2)}) collective-permute-start(bf16[2,4,64,1024]{3,0,2,1:T(2,128)(2,1)S(1)} %dynamic-slice_bitcast_fusion.3), channel_id=1, source_target_pairs={{0,4},{2,6},{4,0},{6,2},{8,12},{10,14},{12,8},{14,10},{16,20},{18,... | collective-permute-start | bytes 3145736 | tf_op jit(solution)/shard_map/ppermute | solution.py:138
  390.9 29.1 %collective-permute-start.30 = (bf16[2,4,64,1024]{3,2,0,1:T(8,128)(2,1)S(1)}, bf16[2,4,64,1024]{3,2,0,1:T(8,128)(2,1)S(1)}, u32[]{:S(2)}, u32[]{:S(2)}) collective-permute-start(bf16[2,4,64,1024]{3,2,0,1:T(8,128)(2,1)S(1)} %bitcast.498), channel_id=1, source_target_pairs={{0,1},{1,0},{2,3},{3,2},{4,5},{5,4},{6,7},{7,6},{8,9},{9,8},{10,11... | collective-permute-start | bytes 3145736 | tf_op jit(solution)/shard_map/ppermute | solution.py:138
  392.4 49.7 %collective-permute-start.8 = (bf16[2,192,256]{2,1,0:T(8,128)(2,1)S(1)}, bf16[2,192,256]{2,1,0:T(8,128)(2,1)S(1)}, u32[]{:S(2)}, u32[]{:S(2)}) collective-permute-start(bf16[2,192,256]{2,1,0:T(8,128)(2,1)S(1)} %fusion.89), channel_id=1, source_target_pairs={{0,1},{1,0},{2,3},{3,2},{4,5},{5,4},{6,7},{7,6},{8,9},{9,8},{10,11... | collective-permute-start | bytes 589832 | tf_op jit(solution)/shard_map/ppermute | solution.py:146
  395.7 35.2 %collective-permute-start.20 = (bf16[4,256,256]{1,2,0:T(8,128)(2,1)S(1)}, bf16[4,256,256]{1,2,0:T(8,128)(2,1)S(1)}, u32[]{:S(2)}, u32[]{:S(2)}) collective-permute-start(bf16[4,256,256]{1,2,0:T(8,128)(2,1)S(1)} %dynamic-slice_bitcast_fusion.8), channel_id=1, source_target_pairs={{0,1},{1,0},{2,3},{3,2},{4,5},{5,4},{6,7},{7,6},{8,9},{9,8},{10,11... | collective-permute-start | bytes 1572872 | tf_op jit(solution)/shard_map/ppermute | solution.py:138
  397.6 33.4 %collective-permute-start.22 = (bf16[4,256,256]{1,2,0:T(8,128)(2,1)S(1)}, bf16[4,256,256]{1,2,0:T(8,128)(2,1)S(1)}, u32[]{:S(2)}, u32[]{:S(2)}) collective-permute-start(bf16[4,256,256]{1,2,0:T(8,128)(2,1)S(1)} %dynamic-slice_bitcast_fusion.7), channel_id=1, source_target_pairs={{0,4},{2,6},{4,0},{6,2},{8,12},{10,14},{12,8},{14,10},{16,20},{18,... | collective-permute-start | bytes 1572872 | tf_op jit(solution)/shard_map/ppermute | solution.py:138
  419.6 17.0 %collective-permute-start.29 = (bf16[4,64,1024]{2,1,0:T(8,128)(2,1)S(1)}, bf16[4,64,1024]{2,1,0:T(8,128)(2,1)S(1)}, u32[]{:S(2)}, u32[]{:S(2)}) collective-permute-start(bf16[4,64,1024]{2,1,0:T(8,128)(2,1)S(1)} %bitcast.511), channel_id=1, source_target_pairs={{0,1},{1,0},{2,3},{3,2},{4,5},{5,4},{6,7},{7,6},{8,9},{9,8},{10,11... | collective-permute-start | bytes 1572872 | tf_op jit(solution)/shard_map/ppermute | solution.py:138
  420.7 17.0 %collective-permute-start.31 = (bf16[4,64,1024]{2,1,0:T(8,128)(2,1)S(1)}, bf16[4,64,1024]{2,1,0:T(8,128)(2,1)S(1)}, u32[]{:S(2)}, u32[]{:S(2)}) collective-permute-start(bf16[4,64,1024]{2,1,0:T(8,128)(2,1)S(1)} %dynamic-slice_bitcast_fusion.6), channel_id=1, source_target_pairs={{0,4},{2,6},{4,0},{6,2},{8,12},{10,14},{12,8},{14,10},{16,20},{18,... | collective-permute-start | bytes 1572872 | tf_op jit(solution)/shard_map/ppermute | solution.py:138
  434.1 31.3 %collective-permute-start.24 = (bf16[2,256,256]{1,2,0:T(8,128)(2,1)}, bf16[2,256,256]{1,2,0:T(8,128)(2,1)S(1)}, u32[]{:S(2)}, u32[]{:S(2)}) collective-permute-start(bf16[2,256,256]{1,2,0:T(8,128)(2,1)} %get-tuple-element.61), channel_id=1, source_target_pairs={{0,16},{2,18},{4,20},{6,22},{8,24},{10,26},{12,28},{14,30},{16,0},... | collective-permute-start | bytes 786440 | tf_op jit(solution)/shard_map/ppermute | solution.py:138
  436.5 28.9 %collective-permute-start.23 = (bf16[2,256,256]{1,2,0:T(8,128)(2,1)}, bf16[2,256,256]{1,2,0:T(8,128)(2,1)}, u32[]{:S(2)}, u32[]{:S(2)}) collective-permute-start(bf16[2,256,256]{1,2,0:T(8,128)(2,1)} %get-tuple-element.60), channel_id=1, source_target_pairs={{0,8},{2,10},{4,12},{6,14},{8,16},{10,18},{12,20},{14,22},{16,24},... | collective-permute-start | bytes 786440 | tf_op jit(solution)/shard_map/ppermute | solution.py:138
  438.8 29.5 %collective-permute-start.34 = (bf16[2,64,1024]{2,1,0:T(8,128)(2,1)}, bf16[2,64,1024]{2,1,0:T(8,128)(2,1)}, u32[]{:S(2)}, u32[]{:S(2)}) collective-permute-start(bf16[2,64,1024]{2,1,0:T(8,128)(2,1)} %get-tuple-element.57), channel_id=1, source_target_pairs={{0,24},{2,26},{4,28},{6,30},{8,0},{10,2},{12,4},{14,6},{16,8},{18,... | collective-permute-start | bytes 786440 | tf_op jit(solution)/shard_map/ppermute | solution.py:138
  442.1 29.1 %collective-permute-start.33 = (bf16[2,64,1024]{2,1,0:T(8,128)(2,1)}, bf16[2,64,1024]{2,1,0:T(8,128)(2,1)}, u32[]{:S(2)}, u32[]{:S(2)}) collective-permute-start(bf16[2,64,1024]{2,1,0:T(8,128)(2,1)} %get-tuple-element.56), channel_id=1, source_target_pairs={{0,16},{2,18},{4,20},{6,22},{8,24},{10,26},{12,28},{14,30},{16,0},... | collective-permute-start | bytes 786440 | tf_op jit(solution)/shard_map/ppermute | solution.py:138
  442.9 28.2 %collective-permute-start.32 = (bf16[2,64,1024]{2,1,0:T(8,128)(2,1)}, bf16[2,64,1024]{2,1,0:T(8,128)(2,1)}, u32[]{:S(2)}, u32[]{:S(2)}) collective-permute-start(bf16[2,64,1024]{2,1,0:T(8,128)(2,1)} %get-tuple-element.55), channel_id=1, source_target_pairs={{0,8},{2,10},{4,12},{6,14},{8,16},{10,18},{12,20},{14,22},{16,24},... | collective-permute-start | bytes 786440 | tf_op jit(solution)/shard_map/ppermute | solution.py:138
  467.2 19.6 %collective-permute-start.26 = (bf16[2,256,256]{1,2,0:T(8,128)(2,1)}, bf16[2,256,256]{1,2,0:T(8,128)(2,1)S(1)}, u32[]{:S(2)}, u32[]{:S(2)}) collective-permute-start(bf16[2,256,256]{1,2,0:T(8,128)(2,1)} %get-tuple-element.21), channel_id=1, source_target_pairs={{0,1},{1,0},{2,3},{3,2},{4,5},{5,4},{6,7},{7,6},{8,9},{9,8},{10,11... | collective-permute-start | bytes 786440 | tf_op jit(solution)/shard_map/ppermute | solution.py:146
  (75 other events, 454.4 us)

commit v2 on v1

--- a/solution.py
+++ b/solution.py
@@ -3,10 +3,13 @@
 import jax
 import jax.numpy as jnp
 from jax import lax
+from jax.experimental import pallas as pl
+from jax.experimental.pallas import tpu as pltpu
 from jax.sharding import PartitionSpec as P
 
 HD = 64
 TEMB = 256
+VMEM_LIMIT = 64 * 1024 * 1024 - 65536
 
 
 def layer_norm(hidden, gain_vec, shift_vec):
@@ -183,6 +186,739 @@
     both = group_scatter(both, out, outer, "seq", out_perm)
     both = group_gather(both, turn, tok_ways, "tok", tok_perm)
     return jnp.transpose(both, (2, 1, 0, 3)).reshape(rows, width).T.astype(jnp.float32)
+
+
+MESH_ID = pl.DeviceIdType.MESH
+BF = jnp.bfloat16
+F32 = jnp.float32
+UNITS = 12
+UNIT_DOWN, UNIT_UP, UNIT_OUT, UNIT_QKV = 0, 4, 8, 9
+ORDERS = "xyxyxyxyxyxy"
+MIB = 1 << 20
+
+
+def mm(left, right, left_dim, right_dim):
+    return lax.dot_general(
+        left, right, (((left_dim,), (right_dim,)), ((), ())), preferred_element_type=F32
+    )
+
+
+def rotated_partner(values):
+    lane = lax.broadcasted_iota(jnp.int32, values.shape, 1)
+    return jnp.where(lane % 64 < 32, pltpu.roll(values, 96, 1), pltpu.roll(values, 32, 1))
+
+
+def backward_kernel(
+    incoming_in,
+    active_in,
+    slope_in,
+    normed_two_in,
+    hidden_one_in,
+    attended_in,
+    qkv_in,
+    normed_one_in,
+    hidden_zero_in,
+    w_down,
+    w_up,
+    w_out,
+    w_qkv,
+    vectors,
+    cosine,
+    sine,
+    mixed_out,
+    tokens_out,
+    shares_out,
+    small_out,
+    partial,
+    core_send,
+    core_recv,
+    recv_one,
+    recv_two,
+    recv_three,
+    weight,
+    wide_a,
+    wide_g,
+    inc,
+    normed,
+    hidden,
+    hidden_z,
+    total,
+    grad_attn,
+    attended,
+    grad_mixed,
+    mixed,
+    message,
+    small_recv,
+    vec_rows,
+    load_sem,
+    weight_sem,
+    core_ssem,
+    core_rsem,
+    credit,
+    one_ssem,
+    one_rsem,
+    two_ssem,
+    two_rsem,
+    three_ssem,
+    three_rsem,
+    gather_ssem,
+    gather_rsem,
+    small_ssem,
+    small_rsem,
+    back_ssem,
+    back_rsem,
+):
+    place, turn = lax.axis_index("seq"), lax.axis_index("tok")
+    core, xx, zz = place % 2, (place // 2) % 2, place // 4
+    yy = turn
+    me = place * 2 + turn
+    devices = 32
+
+    def at_seq(z, x, c):
+        return ((z * 2 + x) * 2 + c, turn)
+
+    core_peer = at_seq(zz, xx, 1 - core)
+    x_peer = at_seq(zz, 1 - xx, core)
+    y_peer = (place, 1 - turn)
+
+    def load(index, source, target):
+        return pltpu.make_async_copy(source, target, load_sem.at[index])
+
+    def load_weight(tile):
+        if tile < 4:
+            source = w_down.at[pl.ds(tile * 1024, 1024), :]
+        elif tile < 8:
+            source = w_up.at[:, pl.ds((tile - 4) * 1024, 1024)]
+        elif tile == 8:
+            source = w_out
+        else:
+            source = w_qkv.at[:, pl.ds((tile - 9) * 1024, 1024)]
+        return pltpu.make_async_copy(source, weight.at[tile % 2], weight_sem.at[tile % 2])
+
+    load(0, incoming_in, inc).start()
+    for part in range(4):
+        columns = pl.ds(part * 1024, 1024)
+        load(1 + part, active_in.at[:, columns], wide_a.at[:, columns]).start()
+    load_weight(0).start()
+    load_weight(1).start()
+    load(5, slope_in, wide_g).start()
+    load(6, hidden_one_in, hidden).start()
+    load(7, normed_two_in, normed).start()
+    load(8, attended_in, attended).start()
+    load(9, hidden_zero_in, hidden_z).start()
+
+    barrier = pltpu.get_barrier_semaphore()
+
+    def greet(step, carry):
+        other = lax.rem(me + step, devices)
+        pl.semaphore_signal(
+            barrier, inc=1, device_id=(other // 2, other % 2), device_id_type=MESH_ID
+        )
+        return carry
+
+    lax.fori_loop(1, devices, greet, 0)
+    pl.semaphore_wait(barrier, devices - 1)
+
+    def remote(source, target, send, recv, device):
+        return pltpu.make_async_remote_copy(
+            src_ref=source,
+            dst_ref=target,
+            send_sem=send,
+            recv_sem=recv,
+            device_id=device,
+            device_id_type=MESH_ID,
+        )
+
+    def core_copy(unit):
+        slot = unit % 4
+        return remote(
+            core_send.at[slot],
+            core_recv.at[slot],
+            core_ssem.at[slot],
+            core_rsem.at[slot],
+            core_peer,
+        )
+
+    def one_copy(unit):
+        if ORDERS[unit] == "x":
+            source, device = partial.at[2 * unit + 1 - xx], x_peer
+        else:
+            source, device = partial.at[pl.ds(2 * unit, 2), 1 - yy], y_peer
+        return remote(
+            source, recv_one.at[unit], one_ssem.at[unit], one_rsem.at[unit], device
+        )
+
+    def two_copy(unit):
+        if ORDERS[unit] == "x":
+            source, device = partial.at[2 * unit + xx, 1 - yy], y_peer
+        else:
+            source, device = partial.at[2 * unit + 1 - xx, yy], x_peer
+        return remote(
+            source, recv_two.at[unit], two_ssem.at[unit], two_rsem.at[unit], device
+        )
+
+    def three_copy(unit, step):
+        other = (zz + step) % 4
+        index = 3 * unit + step - 1
+        return remote(
+            partial.at[2 * unit + xx, yy, other],
+            recv_three.at[unit, step - 1],
+            three_ssem.at[index],
+            three_rsem.at[index],
+            at_seq(other, xx, core),
+        )
+
+    def gather_copy(unit):
+        return remote(
+            shares_out.at[unit, yy],
+            shares_out.at[unit, yy],
+            gather_ssem.at[unit],
+            gather_rsem.at[unit],
+            y_peer,
+        )
+
+    def start_core(unit):
+        if unit >= 4:
+            pl.semaphore_wait(credit.at[unit % 4], 1)
+        core_copy(unit).start()
+
+    def stage_core(unit):
+        core_copy(unit).wait_recv()
+
+        def add(index, carry):
+            x, h, z = index // 8, (index // 4) % 2, index % 4
+            partial[2 * unit + x, h, z] = (
+                partial[2 * unit + x, h, z] + core_recv[unit % 4, x, h, z]
+            )
+            return carry
+
+        lax.fori_loop(0, 16, add, 0)
+        if unit < UNITS - 4:
+            pl.semaphore_signal(
+                credit.at[unit % 4], inc=1, device_id=core_peer, device_id_type=MESH_ID
+            )
+        one_copy(unit).start()
+
+    def stage_one(unit):
+        one_copy(unit).wait_recv()
+
+        def add(index, carry):
+            a, z = index // 4, index % 4
+            if ORDERS[unit] == "x":
+                partial[2 * unit + xx, a, z] = partial[2 * unit + xx, a, z] + recv_one[unit, a, z]
+            else:
+                partial[2 * unit + a, yy, z] = partial[2 * unit + a, yy, z] + recv_one[unit, a, z]
+            return carry
+
+        lax.fori_loop(0, 8, add, 0)
+        two_copy(unit).start()
+
+    def stage_two(unit):
+        two_copy(unit).wait_recv()
+
+        def add(z, carry):
+            partial[2 * unit + xx, yy, z] = partial[2 * unit + xx, yy, z] + recv_two[unit, z]
+            return carry
+
+        lax.fori_loop(0, 4, add, 0)
+        for step in (2, 1, 3):
+            three_copy(unit, step).start()
+
+    def stage_three(unit):
+        value = partial[2 * unit + xx, yy, zz].astype(F32)
+        for step in (1, 2, 3):
+            three_copy(unit, step).wait_recv()
+        for step in (1, 2, 3):
+            value = value + recv_three[unit, step - 1].astype(F32)
+        shares_out[unit, yy] = value.astype(BF)
+        gather_copy(unit).start()
+
+    def stage_gather(unit):
+        gather_copy(unit).wait_recv()
+
+    stages = (stage_core, stage_one, stage_two, stage_three, stage_gather)
+    plan = schedule()
+    cursor = [0]
+
+    def pump(label):
+        while cursor[0] < len(plan):
+            kind, stage, unit = plan[cursor[0]]
+            cursor[0] += 1
+            if kind == "mark":
+                assert stage == label
+                return
+            if stage == -1:
+                start_core(unit)
+            else:
+                stages[stage](unit)
+
+    def wait_sent(units):
+        for unit in units:
+            core_copy(unit).wait_send()
+
+    def place_block(value, unit, x, z):
+        low, high = value[:64], value[64:]
+        own = jnp.where(core == 0, low, high).astype(BF)
+        other = jnp.where(core == 0, high, low).astype(BF)
+        for h in range(2):
+            partial[2 * unit + x, h, z] = own[:, h * 512 : (h + 1) * 512]
+            core_send[unit % 4, x, h, z] = other[:, h * 512 : (h + 1) * 512]
+
+    load(0, incoming_in, inc).wait()
+
+    def down_unit(unit):
+        def step(m, carry):
+            rows = pl.ds(pl.multiple_of(m * 512, 512), 512)
+            value = mm(inc[:, rows], wide_a[:, unit * 1024 : (unit + 1) * 1024], 0, 0)
+            for q in range(4):
+                place_block(value[q * 128 : (q + 1) * 128], unit, q % 2, 2 * m + q // 2)
+            return carry
+
+        lax.fori_loop(0, 2, step, 0)
+
+    for part in range(4):
+        columns = pl.ds(part * 1024, 1024)
+        load(1 + part, active_in.at[:, columns], wide_a.at[:, columns]).wait()
+        down_unit(UNIT_DOWN + part)
+        pump("down%d" % part)
+
+    message[...] = jnp.zeros_like(message)
+    vec_rows[...] = jnp.zeros_like(vec_rows)
+    load(5, slope_in, wide_g).wait()
+    load(6, hidden_one_in, hidden).wait()
+    for tile in range(4):
+        load_weight(tile).wait()
+        columns = slice(tile * 1024, (tile + 1) * 1024)
+
+        def rows_step(m, carry, tile=tile, columns=columns):
+            rows = pl.ds(pl.multiple_of(m * 256, 256), 256)
+            grad = mm(inc[rows, :], weight[tile % 2], 1, 1) * wide_g[rows, columns].astype(F32)
+            grad = grad.astype(BF)
+            wide_g[rows, columns] = grad
+            return carry + jnp.sum(grad.astype(F32), axis=0, keepdims=True)
+
+        sums = lax.fori_loop(0, 2, rows_step, jnp.zeros((1, 1024), F32))
+        for pair in range(2):
+            for row in range(4):
+                at = pair * 512 + row * 128
+                message[2 * tile + pair, 16 + row : 17 + row, :] = sums[:, at : at + 128]
+
+        def mixed_step(m, carry, tile=tile, columns=columns):
+            rows = pl.ds(pl.multiple_of(m * 256, 256), 256)
+            add = mm(wide_a[rows, columns], weight[tile % 2], 1, 0)
+            if tile == 0:
+                total[rows, :] = hidden[rows, :] + vectors[2:3, :] + add
+            elif tile < 3:
+                total[rows, :] = total[rows, :] + add
+            else:
+                mixed[pl.ds(2 * m, 2)] = (total[rows, :] + add).astype(BF).reshape(2, 128, 1024)
+            return carry
+
+        lax.fori_loop(0, 2, mixed_step, 0)
+        load_weight(tile + 2).start()
+        pump("mix%d" % tile)
+    load(10, qkv_in, wide_a.at[:, pl.ds(0, 3072)]).start()
+
+    load(7, normed_two_in, normed).wait()
+    wait_sent(range(0, 4))
+
+    def up_step(p, carry):
+        columns = pl.ds(pl.multiple_of(p * 512, 512), 512)
+        value = mm(wide_g[:, columns], normed[...], 0, 0)
+        for j in range(4):
+            low = value[j * 64 : (j + 1) * 64]
+            high = value[256 + j * 64 : 256 + (j + 1) * 64]
+            place_block(jnp.concatenate([low, high], axis=0), UNIT_UP + j, p % 2, p // 2)
+        return carry
+
+    lax.fori_loop(0, 4, up_step, 0)
+    pump("up0")
+    lax.fori_loop(4, 8, up_step, 0)
+    load(11, normed_one_in, normed).start()
+    pump("up1")
+
+    for tile in range(4, 8):
+        load_weight(tile).wait()
+        columns = slice((tile - 4) * 1024, (tile - 3) * 1024)
+
+        def norm_step(m, carry, tile=tile, columns=columns):
+            rows = pl.ds(pl.multiple_of(m * 256, 256), 256)
+            add = mm(wide_g[rows, columns], weight[tile % 2], 1, 1)
+            total[rows, :] = add if tile == 4 else total[rows, :] + add
+            return carry
+
+        lax.fori_loop(0, 2, norm_step, 0)
+        if tile + 2 < UNITS:
+            load_weight(tile + 2).start()
+        pump("gn%d" % (tile - 4))
+
+    def norm_back(source_ref, gain, rows):
+        h = source_ref[rows, :]
+        center = h - jnp.mean(h, axis=1, keepdims=True)
+        scale = lax.rsqrt(jnp.mean(center * center, axis=1, keepdims=True) + 1e-05)
+        xh = center * scale
+        q = total[rows, :]
+        e = q * gain
+        grad = (
+            e - jnp.mean(e, axis=1, keepdims=True) - xh * jnp.mean(e * xh, axis=1, keepdims=True)
+        ) * scale
+        return (
+            grad,
+            jnp.sum(q * xh, axis=0, keepdims=True),
+            jnp.sum(q, axis=0, keepdims=True),
+        )
+
+    def norm_two_step(m, carry):
+        rows = pl.ds(pl.multiple_of(m * 32, 32), 32)
+        grad, gain_sum, shift_sum = norm_back(hidden, vectors[1:2, :], rows)
+        cot = inc[rows, :].astype(F32)
+        grad = cot + grad
+        hidden[rows, :] = grad
+        grad_attn[rows, :] = grad.astype(BF)
+        return (
+            carry[0] + gain_sum,
+            carry[1] + shift_sum,
+            carry[2] + jnp.sum(cot, axis=0, keepdims=True),
+        )
+
+    none = jnp.zeros((1, 1024), F32)
+    gain_sum, shift_sum, down_sum = lax.fori_loop(0, 16, norm_two_step, (none, none, none))
+    vec_rows[6:7, :] = gain_sum
+    vec_rows[7:8, :] = shift_sum
+    vec_rows[8:9, :] = down_sum
+    pump("ln2")
+
+    load(8, attended_in, attended).wait()
+    wait_sent(range(4, 5))
+
+    def out_step(m, carry):
+        rows = pl.ds(pl.multiple_of(m * 512, 512), 512)
+        value = mm(grad_attn[:, rows], attended[...], 0, 0)
+        for q in range(4):
+            place_block(value[q * 128 : (q + 1) * 128], UNIT_OUT, q % 2, 2 * m + q // 2)
+        return carry
+
+    lax.fori_loop(0, 2, out_step, 0)
+    pump("out")
+    load_weight(8).wait()
+
+    def mixed_back(m, carry):
+        rows = pl.ds(pl.multiple_of(m * 256, 256), 256)
+        grad_mixed[rows, :] = mm(grad_attn[rows, :], weight[0], 1, 1).astype(BF)
+        return carry
+
+    lax.fori_loop(0, 2, mixed_back, 0)
+    load_weight(10).start()
+
+    load(10, qkv_in, wide_a.at[:, pl.ds(0, 3072)]).wait()
+
+    def heads(seq, pair):
+        rows = pl.ds(pl.multiple_of(seq * 128, 128), 128)
+
+        def lanes(base):
+            return pl.ds(pl.multiple_of(base + pair * 128, 128), 128)
+
+        first = lax.broadcasted_iota(jnp.int32, (128, 128), 1) < 64
+        zero = jnp.zeros((128, 128), BF)
+
+        def split(value):
+            return jnp.concatenate(
+                [jnp.where(first, value, zero), jnp.where(first, zero, value)], axis=0
+            )
+
+        q = wide_a[rows, lanes(0)]
+        k_two = split(wide_a[rows, lanes(1024)])
+        v_two = split(wide_a[rows, lanes(2048)])
+        grad_out = grad_mixed[rows, lanes(0)]
+        scores = mm(q, k_two, 1, 1) * 0.125
+        grad_probs = mm(grad_out, v_two, 1, 1)
+        probs, grad_scores = [], []
+        for half in range(2):
+            s = scores[:, half * 128 : (half + 1) * 128]
+            dp = grad_probs[:, half * 128 : (half + 1) * 128]
+            e = jnp.exp(s - jnp.max(s, axis=1, keepdims=True))
+            soft = e / jnp.sum(e, axis=1, keepdims=True)
+            inner = jnp.sum(soft * dp, axis=1, keepdims=True)
+            probs.append(soft.astype(BF))
+            grad_scores.append((soft * (dp - inner)).astype(BF))
+        probs = jnp.concatenate(probs, axis=1)
+        grad_scores = jnp.concatenate(grad_scores, axis=1)
+        grad_q = mm(grad_scores, k_two, 1, 0) * 0.125
+        grad_k = mm(grad_scores, q, 0, 0) * 0.125
+        grad_v = mm(probs, grad_out, 0, 0)
+        grad_k = jnp.where(first, grad_k[:128], grad_k[128:])
+        grad_v = jnp.where(first, grad_v[:128], grad_v[128:])
+
+        def unturn(value):
+            return value * cosine[...] - rotated_partner(value) * sine[...]
+
+        wide_g[rows, lanes(0)] = unturn(grad_q).astype(BF)
+        wide_g[rows, lanes(1024)] = unturn(grad_k).astype(BF)
+        wide_g[rows, lanes(2048)] = grad_v.astype(BF)
+
+    def heads_step(index, carry):
+        heads(index // 8, index % 8)
+        return carry
+
+    for part in range(4):
+        lax.fori_loop(8 * part, 8 * part + 8, heads_step, 0)
+        pump("attn%d" % part)
+
+    load(11, normed_one_in, normed).wait()
+    wait_sent(range(5, 8))
+
+    def qkv_step(p, carry):
+        columns = pl.ds(pl.multiple_of(p * 384, 128), 384)
+        value = mm(wide_g[:, columns], normed[...], 0, 0)
+        for j in range(3):
+            low = value[j * 64 : (j + 1) * 64]
+            high = value[192 + j * 64 : 192 + (j + 1) * 64]
+            place_block(jnp.concatenate([low, high], axis=0), UNIT_QKV + j, p % 2, p // 2)
+        return carry
+
+    lax.fori_loop(0, 8, qkv_step, 0)
+    pump("qkv")
+
+    for tile in range(9, 12):
+        load_weight(tile).wait()
+        columns = slice((tile - 9) * 1024, (tile - 8) * 1024)
+
+        def first_step(m, carry, tile=tile, columns=columns):
+            rows = pl.ds(pl.multiple_of(m * 256, 256), 256)
+            add = mm(wide_g[rows, columns], weight[tile % 2], 1, 1)
+            total[rows, :] = add if tile == 9 else total[rows, :] + add
+            return carry
+
+        lax.fori_loop(0, 2, first_step, 0)
+        if tile == 9:
+            load_weight(11).start()
+    load(9, hidden_zero_in, hidden_z).wait()
+    gain_sum, shift_sum = none, none
+    for seq in range(4):
+
+        def norm_one_step(m, carry, seq=seq):
+            rows = pl.ds(pl.multiple_of(seq * 128 + m * 32, 32), 32)
+            grad, gain_add, shift_add = norm_back(hidden_z, vectors[0:1, :], rows)
+            grad = grad + hidden[rows, :]
+            inc[rows, :] = grad.astype(BF)
+            return (
+                carry[0] + gain_add,
+                carry[1] + shift_add,
+                carry[2] + jnp.sum(grad, axis=0, keepdims=True),
+            )
+
+        gain_sum, shift_sum, embed_sum = lax.fori_loop(
+            0, 4, norm_one_step, (gain_sum, shift_sum, none)
+        )
+        vec_rows[seq : seq + 1, :] = embed_sum
+    vec_rows[4:5, :] = gain_sum
+    vec_rows[5:6, :] = shift_sum
+    for pair in range(8):
+        message[pair, 0:16, :] = vec_rows[:, pair * 128 : (pair + 1) * 128]
+
+    def small_copy(step, other):
+        del step
+        return remote(
+            message.at[other // 4],
+            small_recv.at[me],
+            small_ssem.at[other],
+            small_rsem.at[me],
+            (other // 2, other % 2),
+        )
+
+    def small_start(step, carry):
+        small_copy(step, lax.rem(me + step, devices)).start()
+        return carry
+
+    lax.fori_loop(1, devices, small_start, 0)
+    small_recv[me] = message[place // 2]
+
+    def mixed_back_copies():
+        local = pltpu.make_async_copy(
+            mixed.at[:, pl.ds(yy * 64, 64)], mixed_out.at[pl.ds(yy * 4, 4)], load_sem.at[12]
+        )
+        away = remote(
+            mixed.at[:, pl.ds((1 - yy) * 64, 64)],
+            mixed_out.at[pl.ds(yy * 4, 4)],
+            back_ssem.at[0],
+            back_rsem.at[0],
+            y_peer,
+        )
+        return local, away
+
+    def tokens_back_copies(seq):
+        local = pltpu.make_async_copy(
+            inc.at[pl.ds(seq * 128 + yy * 64, 64)], tokens_out.at[yy * 4 + seq], load_sem.at[13 + seq]
+        )
+        away = remote(
+            inc.at[pl.ds(seq * 128 + (1 - yy) * 64, 64)],
+            tokens_out.at[yy * 4 + seq],
+            back_ssem.at[1 + seq],
+            back_rsem.at[1 + seq],
+            y_peer,
+        )
+        return local, away
+
+    back = [mixed_back_copies()] + [tokens_back_copies(seq) for seq in range(4)]
+    for local, away in back:
+        local.start()
+        away.start()
+
+    pump("end")
+
+    def small_wait(step, carry):
+        source = lax.rem(me + step, devices)
+        pltpu.make_async_remote_copy(
+            src_ref=message.at[0],
+            dst_ref=small_recv.at[source],
+            send_sem=small_ssem.at[source],
+            recv_sem=small_rsem.at[source],
+            device_id=(source // 2, source % 2),
+            device_id_type=MESH_ID,
+        ).wait()
+        return carry
+
+    lax.fori_loop(1, devices, small_wait, 0)
+    small_out[...] = small_recv[...]
+    for local, away in back:
+        local.wait()
+        away.wait()
+    wait_sent(range(8, 12))
+    for unit in range(UNITS):
+        one_copy(unit).wait_send()
+        two_copy(unit).wait_send()
+        for step in (1, 2, 3):
+            three_copy(unit, step).wait_send()
+        gather_copy(unit).wait_send()
+
+
+def schedule():
+    link = 2 / 0.091
+    free = {"x": 0.0, "y": 0.0, "z": 0.0}
+    order, waiting, now = [], [], 0.0
+
+    def send(axis, mbytes, start):
+        free[axis] = max(free[axis], start) + mbytes * link
+        return free[axis] + 1.5
+
+    def run(stage, unit):
+        nonlocal now
+        order.append(("step", stage, unit))
+        now += (0.8, 0.5, 0.3, 0.2, 0.0)[stage]
+        first, second = ("x", "y") if ORDERS[unit] == "x" else ("y", "x")
+        if stage == 0:
+            ready = send(first, 0.524, now)
+        elif stage == 1:
+            ready = send(second, 0.262, now)
+        elif stage == 2:
+            ready = send("z", 0.262, now)
+        elif stage == 3:
+            ready = send("y", 0.0655, now)
+        else:
+            return
+        waiting.append((ready, stage + 1, unit))
+
+    def drain(until):
+        nonlocal now
+        while waiting:
+            waiting.sort()
+            ready, stage, unit = waiting[0]
+            if ready > max(now, until):
+                return
+            waiting.pop(0)
+            now = max(now, ready)
+            run(stage, unit)
+
+    def core(units):
+        for unit in units:
+            order.append(("step", -1, unit))
+            waiting.append((now + 2.5, 0, unit))
+
+    def piece(label, length, units=()):
+        nonlocal now
+        now += length
+        core(units)
+        drain(now)
+        order.append(("mark", label, 0))
+
+    for part in range(4):
+        piece("down%d" % part, 2.0, (UNIT_DOWN + part,))
+    for tile in range(4):
+        piece("mix%d" % tile, 3.6)
+    piece("up0", 3.5)
+    piece("up1", 3.5, range(UNIT_UP, UNIT_UP + 4))
+    for tile in range(4):
+        piece("gn%d" % tile, 1.7)
+    piece("ln2", 2.0)
+    piece("out", 1.8, (UNIT_OUT,))
+    for part in range(4):
+        piece("attn%d" % part, 3.0)
+    piece("qkv", 6.0, range(UNIT_QKV, UNIT_QKV + 3))
+    now += 9.0
+    drain(1e9)
+    order.append(("mark", "end", 0))
+    return order
+
+
+def backward_call(operands, vectors, cosine, sine):
+    vmem = pl.BlockSpec(memory_space=pltpu.VMEM)
+    hbm = pl.BlockSpec(memory_space=pl.ANY)
+    dma = pltpu.SemaphoreType.DMA
+    return pl.pallas_call(
+        backward_kernel,
+        name="backward",
+        out_shape=(
+            jax.ShapeDtypeStruct((8, 64, 1024), BF),
+            jax.ShapeDtypeStruct((8, 64, 1024), BF),
+            jax.ShapeDtypeStruct((UNITS, 2, 64, 512), BF),
+            jax.ShapeDtypeStruct((32, 24, 128), F32),
+        ),
+        in_specs=[hbm] * 13 + [vmem] * 3,
+        out_specs=(hbm, hbm, vmem, vmem),
+        scratch_shapes=[
+            pltpu.VMEM((2 * UNITS, 2, 4, 64, 512), BF),
+            pltpu.VMEM((4, 2, 2, 4, 64, 512), BF),
+            pltpu.VMEM((4, 2, 2, 4, 64, 512), BF),
+            pltpu.VMEM((UNITS, 2, 4, 64, 512), BF),
+            pltpu.VMEM((UNITS, 4, 64, 512), BF),
+            pltpu.VMEM((UNITS, 3, 64, 512), BF),
+            pltpu.VMEM((2, 1024, 1024), BF),
+            pltpu.VMEM((512, 4096), BF),
+            pltpu.VMEM((512, 4096), BF),
+            pltpu.VMEM((512, 1024), BF),
+            pltpu.VMEM((512, 1024), BF),
+            pltpu.VMEM((512, 1024), F32),
+            pltpu.VMEM((512, 1024), F32),
+            pltpu.VMEM((512, 1024), F32),
+            pltpu.VMEM((512, 1024), BF),
+            pltpu.VMEM((512, 1024), BF),
+            pltpu.VMEM((512, 1024), BF),
+            pltpu.VMEM((4, 128, 1024), BF),
+            pltpu.VMEM((8, 24, 128), F32),
+            pltpu.VMEM((32, 24, 128), F32),
+            pltpu.VMEM((16, 1024), F32),
+            dma((17,)),
+            dma((2,)),
+            dma((4,)),
+            dma((4,)),
+            pltpu.SemaphoreType.REGULAR((4,)),
+            dma((UNITS,)),
+            dma((UNITS,)),
+            dma((UNITS,)),
+            dma((UNITS,)),
+            dma((3 * UNITS,)),
+            dma((3 * UNITS,)),
+            dma((UNITS,)),
+            dma((UNITS,)),
+            dma((32,)),
+            dma((32,)),
+            dma((5,)),
+            dma((5,)),
+        ],
+        compiler_params=pltpu.CompilerParams(
+            collective_id=1, has_side_effects=True, vmem_limit_bytes=VMEM_LIMIT
+        ),
+    )(*operands, vectors, cosine, sine)
 
 
 def body(
@@ -303,7 +1039,135 @@
     )
 
 
+def rotary_lanes():
+    cosine, sine = rotary_tables(128)
+    cosine = jnp.tile(cosine[:, 0], (1, 2))
+    sine = jnp.tile(sine[:, 0], (1, 2))
+    sign = jnp.where(jnp.arange(128) % 64 < 32, -1.0, 1.0)
+    return cosine, sine * sign
+
+
+def fast_body(
+    tokens,
+    noise_times,
+    time_proj,
+    time_bias,
+    gain_one,
+    shift_one,
+    w_qkv,
+    w_out,
+    gain_two,
+    shift_two,
+    w_up,
+    b_up,
+    w_down,
+    b_down,
+    cotangent,
+):
+    tok_ways = lax.axis_size("tok")
+    model_width = tokens.shape[-1]
+    seq_count, length = tokens.shape[0] // tok_ways, tokens.shape[1] * tok_ways
+    row_count = seq_count * length
+    all_times = lax.all_gather(noise_times, "seq", tiled=True)
+    own_times = lax.dynamic_slice_in_dim(
+        noise_times, lax.axis_index("tok") * seq_count, seq_count
+    )
+    embed_table = noise_table(own_times).astype(jnp.bfloat16)
+    time_embed = product(embed_table, time_proj) + time_bias.astype(jnp.float32)
+    tokens = gather_sequences(tokens)
+    incoming = gather_sequences(cotangent).reshape(row_count, model_width)
+    hidden_zero = (tokens.astype(jnp.float32) + time_embed[:, None, :]).reshape(
+        row_count, model_width
+    )
+    normed_one = layer_norm(
+        hidden_zero, gain_one.astype(jnp.float32), shift_one.astype(jnp.float32)
+    ).astype(jnp.bfloat16)
+    projected = product(normed_one, w_qkv).astype(jnp.bfloat16)
+    projected = projected.reshape(seq_count, length, 3, 1, model_width)
+    queries, keys_rot, values, _, _ = split_heads(projected)
+    _, attended, _ = attend_items(projected)
+    attended = attended.reshape(row_count, model_width)
+    qkv = jnp.concatenate(
+        [part.reshape(row_count, model_width) for part in (queries, keys_rot, values)], axis=1
+    )
+    hidden_one = hidden_zero + product(attended, w_out)
+    normed_two = layer_norm(
+        hidden_one, gain_two.astype(jnp.float32), shift_two.astype(jnp.float32)
+    ).astype(jnp.bfloat16)
+    upward = product(normed_two, w_up) + b_up.astype(jnp.float32)
+    factor = math.sqrt(2.0 / math.pi)
+    bend = jnp.tanh(factor * (upward + 0.044715 * upward**3))
+    active = (0.5 * upward * (1.0 + bend)).astype(jnp.bfloat16)
+    slope = 0.5 * (1.0 + bend) + 0.5 * upward * (1.0 - bend * bend) * factor * (
+        1.0 + 3.0 * 0.044715 * upward * upward
+    )
+    slope = slope.astype(jnp.bfloat16)
+    vectors = jnp.concatenate(
+        [
+            gain_one[None, :],
+            gain_two[None, :],
+            b_down[None, :],
+            jnp.zeros((5, model_width), jnp.bfloat16),
+        ]
+    ).astype(jnp.float32)
+    cosine, sine = rotary_lanes()
+    mixed_out, grad_tokens, shares, small = backward_call(
+        (
+            incoming,
+            active,
+            slope,
+            normed_two,
+            hidden_one,
+            attended,
+            qkv,
+            normed_one,
+            hidden_zero,
+            w_down,
+            w_up,
+            w_out,
+            w_qkv,
+        ),
+        vectors,
+        cosine,
+        sine,
+    )
+    core = lax.axis_index("seq") % 2
+    shares = jnp.swapaxes(shares, 1, 2).reshape(UNITS, 64, model_width)
+    out_wdown = jnp.swapaxes(shares[0:4], 1, 2).reshape(4 * model_width, 64)
+    out_wup = shares[4:8].reshape(256, model_width).T
+    out_wout = shares[8].T
+    out_wqkv = shares[9:12].reshape(192, model_width).T
+    wide = small[:, 16:20]
+    small = lax.dynamic_slice_in_dim(small[:, :9], core * 64, 64, axis=2)
+    embeds = small[:, :4].reshape(-1, 64)
+    sums = jnp.sum(small[:, 4:], axis=0)
+    out_proj = jnp.dot(
+        noise_table(all_times).astype(jnp.bfloat16).astype(jnp.float32).T,
+        embeds,
+        precision=lax.Precision.HIGHEST,
+    )
+    out_bias = jnp.sum(embeds, axis=0)
+    out_bup = lax.dynamic_slice_in_dim(jnp.sum(wide, axis=0), core * 2, 2, axis=0).reshape(-1)
+    return (
+        mixed_out,
+        grad_tokens,
+        out_proj,
+        out_bias,
+        sums[0],
+        sums[1],
+        out_wqkv.astype(jnp.float32),
+        out_wout.astype(jnp.float32),
+        sums[2],
+        sums[3],
+        out_wup.astype(jnp.float32),
+        out_bup,
+        out_wdown.astype(jnp.float32),
+        sums[4],
+    )
+
+
 def solution(mesh):
+    chosen = fast_body if (mesh.shape["seq"], mesh.shape["tok"]) == (16, 2) else body
     in_specs = (
         P("seq", "tok", None),
         P("seq"),
@@ -337,4 +1201,4 @@
         P(None, "seq"),
         P("seq"),
     )
-    return jax.shard_map(body, mesh=mesh, in_specs=in_specs, out_specs=out_specs, check_vma=False)
+    return jax.shard_map(chosen, mesh=mesh, in_specs=in_specs, out_specs=out_specs, check_vma=False)

time: 509 us -> 308 us (0.61)
  Pallas kernels: 0 us -> 178 us
  local copies, waits for them, and re-layouts: 167 us -> 55.1 us
  matrix products: 93 us -> 20.2 us
  waiting for transfers between devices: 62.9 us -> 0.01 us
  other arithmetic: 84.9 us -> 28.1 us
  starting transfers between devices: 62.5 us -> 8.96 us
  blocking collectives: 28.2 us -> 13.1 us
    pallas_call x0 -> x1, Pallas kernels: none -> 178 us  [backward_call(): pl.pallas_call(backward_kernel, name='backward', out_shape=(jax.ShapeDtyp...]
    dot_general x13 -> x1, matrix products: 61.1 us -> 0.86 us  [fast_body(): jnp.dot(noise_table(all_times).astype(jnp.bfloat16).astype(jnp.float32).T...]
    ppermute x36 -> x0, waiting for transfers between devices: 58.7 us -> none  [the longest x32 48.4 us: group_scatter(): lax.ppermute(piece, axis, perm_of(shift)).astype(jnp.float32)]
    ppermute x36 -> x0, starting transfers between devices: 42 us -> none  [the longest x32 37.2 us: group_scatter(): lax.ppermute(piece, axis, perm_of(shift)).astype(jnp.float32)]
    convert_element_type x36 -> x13, other arithmetic: 49.3 us -> 8.62 us  [the longest x1 3.42 us: split_heads(): split_view[:, :, 0].astype(jnp.float32)]
    dynamic_update_slice x7 -> x0, local copies, waits for them, and re-layouts: 32.2 us -> none  [the longest x4 16.2 us: group_gather(): held = lax.dynamic_update_index_in_dim(held, other, (own - shift) % size, 0)]
    reshape x14 -> x1, local copies, waits for them, and re-layouts: 28.3 us -> 0.57 us  [fast_body(): lax.dynamic_slice_in_dim(jnp.sum(wide, axis=0), core * 2, 2, axis=0)]
    another operation x14 -> x2, other arithmetic: 17.3 us -> 1.05 us
  transfers between devices with their start and end apart: 41 -> 2, of which waited for: 11 -> 0; matrix products, arithmetic and copies ran while one was open for 43% -> 21% of each run, Pallas kernels for 0% -> 0%
where the time goes in v2:
time: 308 us; the launch traced here: 305 us
  Pallas kernels  178 us (58%)
  local copies, waits for them, and re-layouts  55.1 us (18%)
  other arithmetic  28.1 us (9%)
  matrix products  20.2 us (7%)
  blocking collectives  13.1 us (4%)
  starting transfers between devices  8.96 us (3%)
    pallas_call x1, Pallas kernels, backward_call(): pl.pallas_call(backward_kernel, name='backward', out_shape=(jax.ShapeDtyp...  178 us
    unnamed x71, local copies, waits for them, and re-layouts  22.1 us
    dot_general x4, matrix products, product(): return jnp.dot(left_side, right_side, preferred_element_type=jnp.float32)  17.9 us
    unnamed x1, blocking collectives  13.1 us
    all_to_all x2, starting transfers between devices, gather_sequences(): lax.all_to_all(values, 'tok', split_axis=0, concat_axis=1, tiled=True)  8.96 us
    mul x4, local copies, waits for them, and re-layouts, rotate(): return values * cosine + turned * sine_tab  8.09 us
    convert_element_type x2, other arithmetic, split_heads(): rotate(split_view[:, :, 0].astype(jnp.float32), cosine, sine_tab)  7.67 us
  transfers between devices with their start and end apart: 2, of which 0 were waited for; matrix products, arithmetic and copies ran while one was open for 21% of the time, Pallas kernels for 0%

profile of v2, /device:TPU:0, one launch (start us, length us, event | category | flops | bytes accessed | tf_op | source)
XLA Modules:
  0.0 305.1 jit_solution(3780515713077822594)
XLA Ops:
  0.7 4.4 %all-to-all-start.1 = ((bf16[8,64,1024]{2,1,0:T(8,128)(2,1)}), bf16[8,64,1024]{2,1,0:T(8,128)(2,1)S(1)}, u32[]{:S(2)}, u32[]{:S(2)}) async-start(bf16[8,64,1024]{2,1,0:T(8,128)(2,1)} %param.15), calls=%async_computation.1 | async-start | bytes 2097152 | tf_op jit(solution)/shard_map/all_to_all | solution.py:130
  6.0 1.8 copy.106
  10.3 13.1 %all-reduce = s32[128]{0:T(128)S(1)} all-reduce(s32[128]{0:T(128)S(1)} %dynamic-update-slice), channel_id=1, replica_groups=mesh['seq'=16,'tok'=2] {'seq'}, use_global_device_ids=true, to_apply=%add | all-reduce | flops 128 | bytes 1024
  25.9 1.2 convolution_add_fusion.1
  27.1 4.6 %all-to-all-start = ((bf16[8,64,1024]{2,1,0:T(8,128)(2,1)}), bf16[8,64,1024]{2,1,0:T(8,128)(2,1)}, u32[]{:S(2)}, u32[]{:S(2)}) async-start(bf16[8,64,1024]{2,1,0:T(8,128)(2,1)} %param.29), calls=%async_computation | async-start | bytes 2097152 | tf_op jit(solution)/shard_map/all_to_all | solution.py:130
  33.1 1.8 add_convert_fusion.5
  36.7 3.6 %convolution_convert_fusion = bf16[512,3072]{1,0:T(8,128)(2,1)S(1)} fusion(bf16[512,1024]{1,0:T(8,128)(2,1)S(1)} %get-tuple-element.70.normed_one_in, bf16[1024,3072]{1,0:T(8,128)(2,1)S(1)} %bitcast.155), kind=kOutput, calls=%fused_computation.12 | convolution fusion | flops 3222798336 | bytes 10485760 | tf_op jit(solution)/shard_map/dot_general | solution.py:50
  40.3 2.9 copy.99
  43.2 3.8 %reshape_reshape.7 = bf16[4,128,3,16,64]{1,0,4,3,2:T(4,128)(2,1)S(1)} reshape(bf16[512,3072]{0,1:T(8,128)(2,1)} %copy.99) | data formatting | bytes 6291456 | tf_op jit(solution)/shard_map/reshape;reshape | solution.py:64
  47.0 3.4 %slice_convert_fusion.1 = (f32[4,128,1,16,64]{1,0,4,3,2:T(4,128)}, f32[4,128,16,64]{1,0,3,2:T(4,128)S(1)}, f32[4,128,16,64]{1,0,3,2:T(4,128)S(1)}, f32[4,128,1,1...) fusion(bf16[4,128,3,16,64]{1,0,4,3,2:T(4,128)(2,1)S(1)} %reshape_reshape.7), kind=kLoop, calls=%fused_computation.51 | loop fusion | flops 1048576 | bytes 12582912 | tf_op jit(solution)/shard_map/convert_element_type | solution.py:66
  51.2 2.8 add_convert_fusion.4
  54.8 4.0 %fusion.43 = (f32[4,16,128]{2,1,0:T(8,128)S(1)}, f32[4,16,128,128]{2,3,1,0:T(8,128)S(1)}) fusion(f32[4,16,128,128]{2,3,1,0:T(8,128)S(1)} %fusion.21), kind=kOutput, calls=%fused_computation.105 | output fusion | flops 4194431 | bytes 8421376 | tf_op jit(solution)/shard_map/sub | solution.py:82
  61.3 1.4 fusion.44
  62.7 1.3 copy.162
  64.0 1.5 copy.158
  65.5 3.0 copy.107
  68.5 3.1 %copy.156 = f32[128,8,4,128]{3,1,2,0:T(8,128)} copy(f32[128,8,4,128]{3,2,1,0:T(4,128)} %bitcast.152) | data formatting | bytes 4194304
  71.6 2.9 copy.110
  74.5 3.1 %copy.160 = f32[128,8,4,128]{3,1,2,0:T(8,128)} copy(f32[128,8,4,128]{3,2,1,0:T(4,128)} %bitcast.151) | data formatting | bytes 4194304
  77.6 2.9 copy.105
  80.4 3.1 %copy.157 = f32[128,8,4,128]{3,1,2,0:T(8,128)} copy(f32[128,8,4,128]{3,2,1,0:T(4,128)} %bitcast.150) | data formatting | bytes 4194304
  83.5 3.0 copy.108
  86.5 1.2 copy.161
  87.7 2.4 copy.127
  90.1 1.5 copy.114.attended_in
  91.9 2.4 copy.95
  94.4 4.8 %add_convert_fusion.1 = (bf16[512,1024]{1,0:T(8,128)(2,1)S(1)}, bf16[512,1024]{1,0:T(8,128)(2,1)S(1)}) fusion(f32[512,1024]{1,0:T(8,128)} %copy.107, f32[512,1024]{1,0:T(8,128)} %copy.105, f32[512,1024]{1,0:T(8,128)S(1)} %copy-done.3, f32[512,1024]{1,0:T(8,128)} %copy.110, f32[512,1024]{1,0:T(8,128)} %copy.108), kind=kLoop, calls=%fused_computation.34 | loop fusion | flops 3145728 | bytes 12582912 | tf_op jit(solution)/shard_map/convert_element_type | solution.py:66
  99.2 1.8 pad_maximum_fusion.qkv_in
  101.4 11.6 %fusion.8 = (bf16[512,4096]{1,0:T(8,128)(2,1)}, bf16[512,4096]{1,0:T(8,128)(2,1)}) fusion(f32[4096]{0:T(1024)S(1)} %convert_element_type.177, bf16[512,1024]{1,0:T(8,128)(2,1)S(1)} %add_convert_fusion.2.normed_two_in, bf16[1024,4096]{1,0:T(8,128)(2,1)S(1)} %bitcast.143), kind=kOutput, calls=%fused_computation.10 | convolution fusion | flops 4339007488 | bytes 17842176 | tf_op jit(solution)/shard_map/dot_general | solution.py:50
  113.1 177.5 %backward.1 = (bf16[8,64,1024]{2,1,0:T(8,128)(2,1)}, bf16[8,64,1024]{2,1,0:T(8,128)(2,1)}, bf16[12,2,64,512]{3,2,1,0:T(8,128)(2,1)}, f32[32,24,128]{2,1,0:T(8,128)}) custom-call(bf16[512,1024]{1,0:T(8,128)(2,1)} %bitcast.157, bf16[512,4096]{1,0:T(8,128)(2,1)} %get-tuple-element.73.active_in, bf16[512,4096]{1,0:T(8,128)(2,1)} %get-tuple-element.72.slope_in, ...), custom_call_target="tpu_custom_call" | custom-call | tf_op jit(solution)/shard_map/backward/pallas_call | solution.py:867
  290.6 1.4 convert_bitcast_fusion.1
  295.2 1.3 copy.121
  (128 shorter events, 24.5 us)
Async XLA Ops:
  0.6 4.4 %copy-start.16 = (bf16[1024]{0:T(1024)(128)(2,1)S(1)}, bf16[1024]{0:T(1024)(128)(2,1)}, u32[]{:S(2)}) copy-start(bf16[1024]{0:T(1024)(128)(2,1)} %param.19) | copy-start | bytes 6148
  0.7 4.5 %copy-start.17 = (bf16[1024]{0:T(1024)(128)(2,1)S(1)}, bf16[1024]{0:T(1024)(128)(2,1)}, u32[]{:S(2)}) copy-start(bf16[1024]{0:T(1024)(128)(2,1)} %param.23) | copy-start | bytes 6148
  0.7 4.5 %copy-start.18 = (bf16[1024]{0:T(1024)(128)(2,1)S(1)}, bf16[1024]{0:T(1024)(128)(2,1)}, u32[]{:S(2)}) copy-start(bf16[1024]{0:T(1024)(128)(2,1)} %param.18) | copy-start | bytes 6148
  0.7 4.5 %copy-start.19 = (bf16[1024]{0:T(1024)(128)(2,1)S(1)}, bf16[1024]{0:T(1024)(128)(2,1)}, u32[]{:S(2)}) copy-start(bf16[1024]{0:T(1024)(128)(2,1)} %param.20) | copy-start | bytes 6148
  0.7 26.4 %all-to-all-start.1 = ((bf16[8,64,1024]{2,1,0:T(8,128)(2,1)}), bf16[8,64,1024]{2,1,0:T(8,128)(2,1)S(1)}, u32[]{:S(2)}, u32[]{:S(2)}) async-start(bf16[8,64,1024]{2,1,0:T(8,128)(2,1)} %param.15), calls=%async_computation.1 | async-start | bytes 2097152 | tf_op jit(solution)/shard_map/all_to_all | solution.py:130
  6.0 1.9 copy-start.20
  6.0 1.9 copy-start.15
  6.0 2.7 copy-start.21
  6.0 2.8 copy-start.22
  6.0 2.8 copy-start.23
  27.1 64.8 %all-to-all-start = ((bf16[8,64,1024]{2,1,0:T(8,128)(2,1)}), bf16[8,64,1024]{2,1,0:T(8,128)(2,1)}, u32[]{:S(2)}, u32[]{:S(2)}) async-start(bf16[8,64,1024]{2,1,0:T(8,128)(2,1)} %param.29), calls=%async_computation | async-start | bytes 2097152 | tf_op jit(solution)/shard_map/all_to_all | solution.py:130
  32.6 3.3 %slice-start.2 = ((s8[6291456]{0:T(1024)(128)(4,1)}), s8[4194304]{0:T(1024)(128)(4,1)S(1)}, s32[]{:S(2)}) async-start(s8[6291456]{0:T(1024)(128)(4,1)} %bitcast.154), calls=%async_computation.4 | async-start | bytes 8388608
  32.9 3.8 %slice-start.3 = ((s8[6291456]{0:T(1024)(128)(4,1)}), s8[2097152]{0:T(1024)(128)(4,1)S(1)}, s32[]{:S(2)}) async-start(s8[6291456]{0:T(1024)(128)(4,1)} %bitcast.154), calls=%async_computation.5 | async-start | bytes 4194304
  35.0 1.0 copy-start.7
  50.4 8.4 %copy-start.4 = (bf16[4,128,1,16,64]{1,0,4,3,2:T(4,128)(2,1)}, bf16[4,128,1,16,64]{1,0,4,3,2:T(4,128)(2,1)S(1)}, u32[]{:S(2)}) copy-start(bf16[4,128,1,16,64]{1,0,4,3,2:T(4,128)(2,1)S(1)} %get-tuple-element.80) | copy-start | bytes 3145732
  58.9 1.6 copy-start.2
  59.6 1.8 copy-start.1
  62.7 38.3 %copy-start = (f32[512,1024]{1,0:T(8,128)}, f32[512,1024]{1,0:T(8,128)S(1)}, u32[]{:S(2)}) copy-start(f32[512,1024]{1,0:T(8,128)S(1)} %get-tuple-element.103.hidden_one_in) | copy-start | bytes 6291460
  83.5 3.0 copy-start.5
  87.7 2.4 copy-start.8
  91.9 2.4 copy-start.3
  91.9 9.5 %slice-start = ((s8[8388608]{0:T(1024)(128)(4,1)}), s8[4194304]{0:T(1024)(128)(4,1)S(1)}, s32[]{:S(2)}) async-start(s8[8388608]{0:T(1024)(128)(4,1)} %bitcast.142), calls=%async_computation.2 | async-start | bytes 8388608
  94.4 4.9 %copy-start.9 = (bf16[512,1024]{1,0:T(8,128)(2,1)S(1)}, bf16[512,1024]{1,0:T(8,128)(2,1)}, u32[]{:S(2)}) copy-start(bf16[512,1024]{1,0:T(8,128)(2,1)} %copy.127) | copy-start | bytes 3145732
  94.4 7.1 %slice-start.1 = ((s8[8388608]{0:T(1024)(128)(4,1)}), s8[4194304]{0:T(1024)(128)(4,1)S(1)}, s32[]{:S(2)}) async-start(s8[8388608]{0:T(1024)(128)(4,1)} %bitcast.142), calls=%async_computation.3 | async-start | bytes 8388608
  101.4 11.7 %copy-start.6 = (bf16[512,1024]{1,0:T(8,128)(2,1)}, bf16[512,1024]{1,0:T(8,128)(2,1)S(1)}, u32[]{:S(2)}) copy-start(bf16[512,1024]{1,0:T(8,128)(2,1)S(1)} %add_convert_fusion.2.normed_two_in) | copy-start | bytes 3145732
  290.6 3.5 %copy-start.12 = (f32[32,24,128]{2,1,0:T(8,128)S(1)}, f32[32,24,128]{2,1,0:T(8,128)}, u32[]{:S(2)}) copy-start(f32[32,24,128]{2,1,0:T(8,128)} %get-tuple-element.20) | copy-start | bytes 1179652
  297.7 4.4 %copy-start.13 = (bf16[128,128]{1,0:T(8,128)(2,1)S(1)}, bf16[128,128]{1,0:T(8,128)(2,1)}, u32[]{:S(2)}) copy-start(bf16[128,128]{1,0:T(8,128)(2,1)} %get-tuple-element.96) | copy-start | bytes 98308
  297.7 4.4 %copy-start.14 = (bf16[128,128]{1,0:T(8,128)(2,1)S(1)}, bf16[128,128]{1,0:T(8,128)(2,1)}, u32[]{:S(2)}) copy-start(bf16[128,128]{1,0:T(8,128)(2,1)} %get-tuple-element.97) | copy-start | bytes 98308
  297.7 5.3 %copy-start.11 = (bf16[8,64,1024]{2,1,0:T(8,128)(2,1)S(1)}, bf16[8,64,1024]{2,1,0:T(8,128)(2,1)}, u32[]{:S(2)}) copy-start(bf16[8,64,1024]{2,1,0:T(8,128)(2,1)} %get-tuple-element.120) | copy-start | bytes 3145732
  299.3 4.6 %copy-start.10 = (bf16[8,64,1024]{2,1,0:T(8,128)(2,1)S(1)}, bf16[8,64,1024]{2,1,0:T(8,128)(2,1)}, u32[]{:S(2)}) copy-start(bf16[8,64,1024]{2,1,0:T(8,128)(2,1)} %get-tuple-element.121) | copy-start | bytes 3145732
